TPU v7x, 32 devices: a whole 2x2x4 slice. The times are simulated.
32 devices in a mesh: ctx: 8 (over y, x, core), head: 4 (over z).
Axes of the slice: x: 2, y: 2, z: 4, core: 2. Of those that a mesh axis runs over, the one named last changes fastest.
Arguments:
- queries: bfloat16 [8192, 4096], P('ctx', 'head'), may hold values from -100 to 100
- keys: bfloat16 [8192, 4096], P('ctx', 'head'), may hold values from -5 to 5
- values: bfloat16 [8192, 4096], P('ctx', 'head'), may hold values from -12 to 12
- block_perm: int32 [32, 32], P('head'), may hold values from 0 to 31, as said below
- norm_gain: float32 [4096], P('head'), may hold values from 0.5 to 1.5
Outputs:
- normalized: bfloat16 [8192, 4096], P('ctx', 'head')
Inputs may be any that keep to these rules, and one draw needn't show every extreme that they name: `block_perm`: each row is a permutation of the 32 blocks. With the blocks of one index of ctx being 4 consecutive blocks: in one head, at most one query block of one ctx index matches a key block of one given ctx index; over the 8 consecutive heads of one head group, at most 4 do, and some pairs of ctx indices reach 4 in every group.
All inputs are finite; a program needn't handle non-finite values.
Results may differ from a plain program's by a relative error of at most 0.0046.
Values may be sent and summed in bfloat16 or wider, within the bound.
No kernel may reach another device: no remote copies, remote signals or barrier semaphores. Data moves between devices by JAX's collectives and lax.ppermute only.
A program may use at most 128 MiB of HBM per device.

v0:
```python
import functools
import math

import jax
import jax.numpy as jnp
from jax import lax
from jax.experimental import pallas as pl
from jax.experimental.pallas import tpu as pltpu
from jax.sharding import PartitionSpec as P

NORM_EPS = 1e-06
ANY = pl.BlockSpec(memory_space=pl.ANY)
SMEM = pl.BlockSpec(memory_space=pltpu.SMEM)
VMEM = pl.BlockSpec(memory_space=pltpu.VMEM)
PARAMS = pltpu.CompilerParams(vmem_limit_bytes=16 * 1024 * 1024)
CONTRACT_LAST = (((1,), (1,)), ((), ()))


class Sizes:
    def __init__(self, queries, block_perm):
        self.ctx = lax.axis_size("ctx")
        self.heads = block_perm.shape[0]
        self.blocks = block_perm.shape[1] // self.ctx
        self.tokens, self.width = queries.shape
        self.block_len = self.tokens // self.blocks
        self.head_dim = self.width // self.heads
        self.capacity = self.heads // 2
        self.full = self.ctx * self.capacity == self.heads * self.blocks
        self.exponent = math.log2(math.e) / math.sqrt(self.head_dim)

    def tile(self, block, head):
        rows = pl.ds(pl.multiple_of(block * self.block_len, self.block_len), self.block_len)
        return rows, pl.ds(pl.multiple_of(head * self.head_dim, self.head_dim), self.head_dim)

    def send_shape(self):
        return (2, self.capacity, self.block_len, self.head_dim)


def schedule(ctx):
    if ctx == 8:
        steps = [("base", [2]), ("prev", [5]), ((0, 1), [3])]
        return [6, 7, 4, 1], steps + [((d,), []) for d in (6, 7, 4, 2)] + [((5, 3), [])]
    rest = list(range(1, ctx))
    return rest, [("base", []), ("prev", []), ((0,), [])] + [((d,), []) for d in rest]


def near(array):
    return pltpu.with_memory_space_constraint(array, pltpu.VMEM)


def far(array):
    return pltpu.with_memory_space_constraint(array, pltpu.HBM)


def wanted(sizes, d, rank, perm):
    start = jnp.bitwise_xor(rank, d) * sizes.blocks
    slot = jnp.int32(0)
    for head in range(sizes.heads):
        found = jnp.int32(-1)
        for j in range(sizes.blocks):
            source = perm[head, start + j] - rank * sizes.blocks
            found = jnp.where((source >= 0) & (source < sizes.blocks), source, found)
        yield head, found, slot
        slot = slot + (found >= 0).astype(jnp.int32)


def pack_near(sizes, items, which, array, send):
    for head, found, slot in items:

        @pl.when(found >= 0)
        def _():
            send[which, slot] = array[sizes.tile(found, head)]


def pack_both(sizes, d, rank, perm, keys, values, send):
    items = list(wanted(sizes, d, rank, perm))
    for which, array in enumerate((keys, values)):
        pack_near(sizes, items, which, array, send)


def first_kernel(
    sizes, partners, rank_ref, perm_far, keys, values, near_keys, near_values, last, *rest
):
    sends, (perm, perm_sem, sems) = rest[:-3], rest[-3:]
    perm_copy = pltpu.make_async_copy(perm_far, perm, perm_sem.at[0])
    perm_copy.start()
    copies = [
        pltpu.make_async_copy(keys, near_keys, sems.at[0]),
        pltpu.make_async_copy(values, near_values, sems.at[1]),
    ]
    for copy in copies:
        copy.start()
    perm_copy.wait()
    found = [list(wanted(sizes, d, rank_ref[0], perm)) for d in partners]
    for i, (copy, array) in enumerate(zip(copies, (near_keys, near_values))):
        copy.wait()
        last[i] = array[sizes.tokens - sizes.block_len :]
        for items, send in zip(found, sends):
            pack_near(sizes, items, i, array, send)


def first_sends(sizes, partners, rank, perm, keys, values):
    near_keys, near_values, last, *sends = pl.pallas_call(
        functools.partial(first_kernel, sizes, partners),
        out_shape=[pltpu.VMEM(keys.shape, keys.dtype)] * 2
        + [pltpu.VMEM((2, sizes.block_len, sizes.width), keys.dtype)]
        + [pltpu.VMEM(sizes.send_shape(), keys.dtype)] * len(partners),
        in_specs=[SMEM, ANY, ANY, ANY],
        out_specs=[VMEM] * (3 + len(partners)),
        scratch_shapes=[
            pltpu.SMEM(perm.shape, perm.dtype),
            pltpu.SemaphoreType.DMA((1,)),
            pltpu.SemaphoreType.DMA((2,)),
        ],
        compiler_params=PARAMS,
        cost_estimate=pl.CostEstimate(flops=1, bytes_accessed=1, transcendentals=0),
        name="first_sends",
    )(rank, far(perm), far(keys), far(values))
    return near_keys, near_values, last, dict(zip(partners, sends))


def weigh(sizes, scores, peak, values):
    weights = jnp.exp2((scores - peak) * sizes.exponent).astype(jnp.bfloat16)
    ones = jnp.ones(values.shape, values.dtype)
    both = jnp.concatenate([values, ones], axis=1)
    return jnp.dot(weights, both, preferred_element_type=jnp.float32)


def list_matches(sizes, rank, perm, table, counts):
    for d in range(sizes.ctx):
        counts[d] = 0
        if not sizes.full:
            for c in range(sizes.capacity):
                table[d * sizes.capacity + c] = -1
    for head in range(sizes.heads):
        for j in range(sizes.blocks):
            source = perm[head, rank * sizes.blocks + j]
            d = jnp.bitwise_xor(lax.div(source, sizes.blocks), rank)
            slot = counts[d]
            counts[d] = slot + 1
            table[d * sizes.capacity + slot] = (head * sizes.blocks + j) * sizes.blocks + lax.rem(
                source, sizes.blocks
            )


def base_kernel(sizes, partners, rank_ref, perm, queries, keys, values, *rest):
    near_queries, mixture, weight_sum, peaks, squares, table, *sends = rest[: 6 + len(partners)]
    counts, sem = rest[6 + len(partners) :]
    copy = pltpu.make_async_copy(queries, near_queries, sem.at[0])
    copy.start()
    rank = rank_ref[0]
    for d, send in zip(partners, sends):
        pack_both(sizes, d, rank, perm, keys, values, send)
    list_matches(sizes, rank, perm, table, counts)
    squares[...] = jnp.zeros_like(squares)
    copy.wait()
    n = sizes.block_len

    def one_head(head, _):
        columns = sizes.tile(0, head)[1]
        for j in range(sizes.blocks):
            here = slice(j * n, (j + 1) * n), columns
            context = slice(max(j - 1, 0) * n, (j + 1) * n), columns
            scores = lax.dot_general(
                near_queries[here],
                keys[context],
                CONTRACT_LAST,
                preferred_element_type=jnp.float32,
            )
            row = lax.broadcasted_iota(jnp.int32, (n, n), 0)
            column = lax.broadcasted_iota(jnp.int32, (n, n), 1)
            own = jnp.where(row >= column, scores[:, -n:], -jnp.inf)
            scores = own if j == 0 else jnp.concatenate([scores[:, :n], own], axis=1)
            peak = jnp.max(scores, axis=1, keepdims=True)
            total = weigh(sizes, scores, peak, values[context])
            mixture[here] = total[:, : sizes.head_dim]
            weight_sum[here] = total[:, sizes.head_dim :]
            peaks[here] = jnp.broadcast_to(peak, (n, sizes.head_dim))
        return 0

    lax.fori_loop(0, sizes.heads, one_head, 0)


def base(sizes, partners, rank, perm, queries, keys, values):
    state = pltpu.VMEM((sizes.tokens, sizes.width), jnp.float32)
    count = sizes.heads * sizes.blocks
    near_queries, *rest = pl.pallas_call(
        functools.partial(base_kernel, sizes, partners),
        out_shape=[
            pltpu.VMEM(queries.shape, queries.dtype),
            state,
            state,
            state,
            pltpu.VMEM((sizes.tokens, sizes.head_dim), jnp.float32),
            jax.ShapeDtypeStruct((sizes.ctx * sizes.capacity,), jnp.int32),
        ]
        + [pltpu.VMEM(sizes.send_shape(), keys.dtype)] * len(partners),
        in_specs=[SMEM, SMEM, ANY, VMEM, VMEM],
        out_specs=[VMEM] * 5 + [SMEM] + [VMEM] * len(partners),
        scratch_shapes=[
            pltpu.SMEM((sizes.ctx,), jnp.int32),
            pltpu.SemaphoreType.DMA((1,)),
        ],
        compiler_params=PARAMS,
        cost_estimate=pl.CostEstimate(flops=1, bytes_accessed=1, transcendentals=0),
        name="base_items",
    )(rank, perm, far(queries), near(keys), near(values))
    return near_queries, tuple(rest[:4]), rest[4], dict(zip(partners, rest[5:]))


def update_kernel(sizes, group, partners, last, rank_ref, perm, table, queries, keys, values, *rest):
    before = group == "prev"
    remote = ["prev"] if before else [d for d in group if d > 0]
    received, rest = dict(zip(remote, rest)), rest[len(remote) + 4 :]
    mixture, weight_sum, peaks, squares = rest[:4]
    rank = rank_ref[0]
    for d, send in zip(partners, rest[4:]):
        pack_both(sizes, d, rank, perm, keys, values, send)

    def add(here, key_tile, value_tile):
        scores = lax.dot_general(
            queries[here], key_tile, CONTRACT_LAST, preferred_element_type=jnp.float32
        )
        old = peaks[here]
        new = jnp.maximum(old, jnp.max(scores, axis=1, keepdims=True))
        wide = jnp.concatenate([new] * (sizes.block_len // sizes.head_dim), axis=1)
        total = weigh(sizes, scores, wide, value_tile)
        shrink = jnp.exp2((old - new) * sizes.exponent)
        mixed = mixture[here] * shrink + total[:, : sizes.head_dim]
        summed = weight_sum[here] * shrink + total[:, sizes.head_dim :]
        if before:
            mixture[here] = mixed
            weight_sum[here] = summed
            peaks[here] = new
        else:
            attended = mixed / summed
            mixture[here] = attended
            squares[here[0]] += attended * attended

    if before:

        @pl.when(rank > 0)
        def _():
            for head in range(sizes.heads):
                here = sizes.tile(0, head)
                add(here, *[received["prev"][i, :, here[1]] for i in range(2)])

        return

    def match(d, c, item):
        head = lax.div(item, sizes.blocks * sizes.blocks)
        here = sizes.tile(lax.rem(lax.div(item, sizes.blocks), sizes.blocks), head)
        if d > 0:
            add(here, received[d][0, c], received[d][1, c])
        else:
            there = sizes.tile(lax.rem(item, sizes.blocks), head)
            add(here, keys[there], values[there])

    for d in group:
        for c in range(sizes.capacity):
            item = table[d * sizes.capacity + c]
            if sizes.full:
                match(d, c, item)
            else:
                pl.when(item >= 0)(functools.partial(match, d, c, item))
    if last:
        rest[4][...] = lax.dot_general(
            jnp.ones((8, sizes.head_dim), jnp.float32),
            squares[...],
            CONTRACT_LAST,
            precision=lax.Precision.HIGHEST,
            preferred_element_type=jnp.float32,
        )[:1]


def update(sizes, group, partners, last, rank, perm, table, queries, keys, values, received, state):
    remote = [received["prev"]] if group == "prev" else [received[d] for d in group if d > 0]
    arrays = [near(a) for a in [queries, keys, values] + remote + list(state)]
    count = sizes.heads if group == "prev" else len(group) * sizes.capacity
    out_shape = [pltpu.VMEM(a.shape, a.dtype) for a in state]
    out_shape += [pltpu.VMEM(sizes.send_shape(), keys.dtype)] * len(partners)
    if last:
        out_shape.append(jax.ShapeDtypeStruct((1, sizes.tokens), jnp.float32))
    first_state = 3 + len(arrays) - len(state)
    out = pl.pallas_call(
        functools.partial(update_kernel, sizes, group, partners, last),
        out_shape=out_shape,
        in_specs=[SMEM] * 3 + [VMEM] * len(arrays),
        out_specs=[VMEM] * len(out_shape),
        input_output_aliases={first_state + i: i for i in range(len(state))},
        compiler_params=PARAMS,
        cost_estimate=pl.CostEstimate(flops=1, bytes_accessed=1, transcendentals=0),
        name="update_items",
    )(rank, perm, table, *arrays)
    return tuple(out[:4]), out[4:]


def scale_kernel(width, block_len, gain, *rest):
    sums, (attended, out, buffer, sems) = rest[:-4], rest[-4:]
    total = sums[0][...]
    for other in sums[1:]:
        total = total + other[...]
    inverse = lax.rsqrt(total / width + NORM_EPS)
    steps = attended.shape[0] // block_len
    copies = []
    for i in range(steps):
        rows = slice(i * block_len, (i + 1) * block_len)
        column = jnp.transpose(jnp.broadcast_to(inverse[:, rows], (8, block_len)))[:, :1]
        buffer[rows] = (attended[rows] * column * gain[...]).astype(out.dtype)
        copies.append(pltpu.make_async_copy(buffer.at[rows], out.at[rows], sems.at[i]))
        copies[i].start()
    for copy in copies:
        copy.wait()


def scaled(attended, sums, gain, width, block_len):
    tok_rows, row_width = attended.shape
    return pl.pallas_call(
        functools.partial(scale_kernel, width, block_len),
        out_shape=jax.ShapeDtypeStruct((tok_rows, row_width), jnp.bfloat16),
        in_specs=[VMEM] * (len(sums) + 2),
        out_specs=ANY,
        scratch_shapes=[
            pltpu.VMEM((tok_rows, row_width), jnp.bfloat16),
            pltpu.SemaphoreType.DMA((tok_rows // block_len,)),
        ],
        compiler_params=PARAMS,
        name="scale_rows",
    )(gain.reshape(1, row_width), *sums, near(attended))


def per_device(queries, keys, values, block_perm, norm_gain):
    sizes = Sizes(queries, block_perm)
    head_size = lax.axis_size("head")
    rank = lax.axis_index("ctx").astype(jnp.int32).reshape(1)
    received = {}

    def exchange(sends):
        for d, array in sends.items():
            with jax.named_scope(f"match{d}"):
                route = [(i, i ^ d) for i in range(sizes.ctx)]
                received[d] = lax.ppermute(array, "ctx", route)

    first, steps = schedule(sizes.ctx)
    keys, values, last_block, sends = first_sends(sizes, first, rank, block_perm, keys, values)
    with jax.named_scope("previous"):
        route = [(i, i + 1) for i in range(sizes.ctx - 1)]
        received["prev"] = lax.ppermute(last_block, "ctx", route)
    exchange(sends)
    queries, state, table, sends = base(
        sizes, steps[0][1], rank, block_perm, queries, keys, values
    )
    exchange(sends)
    for group, partners in steps[1:]:
        last = group == steps[-1][0]
        state, extra = update(
            sizes, group, partners, last, rank, block_perm, table, queries, keys, values,
            received, state,
        )
        exchange(dict(zip(partners, extra)))
    sums = [extra[-1]]
    for d in range(1, head_size):
        sums.append(lax.ppermute(sums[0], "head", [(i, i ^ d) for i in range(head_size)]))
    return scaled(state[0], sums, norm_gain, sizes.width * head_size, sizes.block_len)


def solution(mesh):
    placed = (P("ctx", "head"), P("ctx", "head"), P("ctx", "head"), P("head", None), P("head"))
    return jax.shard_map(
        per_device, mesh=mesh, in_specs=placed, out_specs=P("ctx", "head"), check_vma=False
    )
```

profile of v0, /device:TPU:0, one launch (start us, length us, event | category | flops | bytes accessed | tf_op | source)
XLA Modules:
  0.0 78.7 jit_solution(7391881145021655610)
XLA Ops:
  0.0 2.8 %first_sends.1 = (bf16[1024,1024]{1,0:T(8,128)(2,1)S(1)}, bf16[1024,1024]{1,0:T(8,128)(2,1)S(1)}, bf16[2,256,1024]{2,1,0:T(8,128)(2,1)S(1)}, bf16[2,4,256,128]{3...) custom-call(s32[1]{0:T(128)} %bitcast.1.rank_ref, ...), custom_call_target="tpu_custom_call" | custom-call | flops 1 | bytes 1 | tf_op jit(solution)/shard_map/first_sends/pallas_call | solution.py:103
  2.8 2.4 %collective-permute-start = (bf16[2,256,1024]{2,1,0:T(8,128)(2,1)S(1)}, bf16[2,256,1024]{2,1,0:T(8,128)(2,1)S(1)}, u32[]{:S(2)}, u32[]{:S(2)}) collective-permute-start(bf16[2,256,1024]{2,1,0:T(8,128)(2,1)S(1)} %get-tuple-element.51), channel_id=1, source_target_pairs={{0,4},{4,8},{8,12},{12,16},{16,20},{20,24},{24,28},{1,5},{5,9},{9,... | collective-permute-start | bytes 3145736 | tf_op jit(solution)/shard_map/previous/ppermute | solution.py:348
  5.2 2.6 %collective-permute-start.2 = (bf16[2,4,256,128]{3,2,1,0:T(8,128)(2,1)S(1)}, bf16[2,4,256,128]{3,2,1,0:T(8,128)(2,1)S(1)}, u32[]{:S(2)}, u32[]{:S(2)}) collective-permute-start(bf16[2,4,256,128]{3,2,1,0:T(8,128)(2,1)S(1)} %get-tuple-element.57), channel_id=1, source_target_pairs={{0,4},{4,0},{8,12},{12,8},{16,20},{20,16},{24,28},{28,24},{1,5},{5... | collective-permute-start | bytes 1572872 | tf_op jit(solution)/shard_map/match1/ppermute | solution.py:342
  7.8 0.9 %collective-permute-start.7 = (bf16[2,4,256,128]{3,2,1,0:T(8,128)(2,1)S(1)}, bf16[2,4,256,128]{3,2,1,0:T(8,128)(2,1)S(1)}, u32[]{:S(2)}, u32[]{:S(2)}) collective-permute-start(bf16[2,4,256,128]{3,2,1,0:T(8,128)(2,1)S(1)} %get-tuple-element.66), channel_id=1, source_target_pairs={{0,24},{4,28},{8,16},{12,20},{16,8},{20,12},{24,0},{28,4},{1,25},{... | collective-permute-start | bytes 1572872 | tf_op jit(solution)/shard_map/match6/ppermute | solution.py:342
  8.8 2.0 %collective-permute-start.5 = (bf16[2,4,256,128]{3,2,1,0:T(8,128)(2,1)S(1)}, bf16[2,4,256,128]{3,2,1,0:T(8,128)(2,1)S(1)}, u32[]{:S(2)}, u32[]{:S(2)}) collective-permute-start(bf16[2,4,256,128]{3,2,1,0:T(8,128)(2,1)S(1)} %get-tuple-element.64), channel_id=1, source_target_pairs={{0,16},{4,20},{8,24},{12,28},{16,0},{20,4},{24,8},{28,12},{1,17},{... | collective-permute-start | bytes 1572872 | tf_op jit(solution)/shard_map/match4/ppermute | solution.py:342
  10.8 0.6 collective-permute-start.6
  11.4 10.8 %base_items.1 = (bf16[1024,1024]{1,0:T(8,128)(2,1)S(1)}, f32[1024,1024]{1,0:T(8,128)S(1)}, f32[1024,1024]{1,0:T(8,128)S(1)}, f32[1024,1024]{1,0:T(8,128)S(1)}, f...) custom-call(s32[1]{0:T(128)} %bitcast.1.rank_ref, s32[8,32]{1,0:T(8,128)S(1)} %copy-done, ...), custom_call_target="tpu_custom_call" | custom-call | flops 1 | bytes 1 | tf_op jit(solution)/shard_map/base_items/pallas_call | solution.py:187
  22.2 0.0 collective-permute-done.rest_0_
  22.2 9.1 %collective-permute-start.4 = (bf16[2,4,256,128]{3,2,1,0:T(8,128)(2,1)S(1)}, bf16[2,4,256,128]{3,2,1,0:T(8,128)(2,1)S(1)}, u32[]{:S(2)}, u32[]{:S(2)}) collective-permute-start(bf16[2,4,256,128]{3,2,1,0:T(8,128)(2,1)S(1)} %get-tuple-element.63), channel_id=1, source_target_pairs={{0,8},{4,12},{8,0},{12,4},{16,24},{20,28},{24,16},{28,20},{1,9},{5... | collective-permute-start | bytes 1572872 | tf_op jit(solution)/shard_map/match2/ppermute | solution.py:342
  31.3 0.9 %update_items.7 = (f32[1024,1024]{1,0:T(8,128)S(1)}, f32[1024,1024]{1,0:T(8,128)S(1)}, f32[1024,1024]{1,0:T(8,128)S(1)}, f32[1024,128]{1,0:T(8,128)S(1)}, bf16[2,4,256,128]{3,2,1,0:T(8,128)(2,1)S(1)}) custom-call(s32[1]{0:T(128)} %bitcast.1.rank_ref, s32[8,32]{1,0:T(8,128)S(1)} %copy-done, ...), custom_call_target="tpu_custom_call", output_to_operand_aliasing={{0}: (7, {}), {1}: (8, {}), {2}: (9, {}), {3}: (10, {})} | custom-call | flops 1 | bytes 1 | tf_op jit(solution)/shard_map/update_items/pallas_call | solution.py:285
  32.2 0.0 collective-permute-done.2.rest_0_
  32.2 0.1 collective-permute-start.1
  32.3 2.3 %update_items.8 = (f32[1024,1024]{1,0:T(8,128)S(1)}, f32[1024,1024]{1,0:T(8,128)S(1)}, f32[1024,1024]{1,0:T(8,128)S(1)}, f32[1024,128]{1,0:T(8,128)S(1)}, bf16[2,4,256,128]{3,2,1,0:T(8,128)(2,1)S(1)}) custom-call(s32[1]{0:T(128)} %bitcast.1.rank_ref, s32[8,32]{1,0:T(8,128)S(1)} %copy-done, ...), custom_call_target="tpu_custom_call", output_to_operand_aliasing={{0}: (7, {}), {1}: (8, {}), {2}: (9, {}), {3}: (10, {})} | custom-call | flops 1 | bytes 1 | tf_op jit(solution)/shard_map/update_items/pallas_call | solution.py:285
  34.7 0.0 collective-permute-done.7.rest_0_
  34.7 7.8 %collective-permute-start.3 = (bf16[2,4,256,128]{3,2,1,0:T(8,128)(2,1)S(1)}, bf16[2,4,256,128]{3,2,1,0:T(8,128)(2,1)S(1)}, u32[]{:S(2)}, u32[]{:S(2)}) collective-permute-start(bf16[2,4,256,128]{3,2,1,0:T(8,128)(2,1)S(1)} %get-tuple-element.62), channel_id=1, source_target_pairs={{0,12},{4,8},{8,4},{12,0},{16,28},{20,24},{24,20},{28,16},{1,13},{... | collective-permute-start | bytes 1572872 | tf_op jit(solution)/shard_map/match3/ppermute | solution.py:342
  42.5 1.3 %update_items.9 = (f32[1024,1024]{1,0:T(8,128)S(1)}, f32[1024,1024]{1,0:T(8,128)S(1)}, f32[1024,1024]{1,0:T(8,128)S(1)}, f32[1024,128]{1,0:T(8,128)S(1)}) custom-call(s32[1]{0:T(128)} %bitcast.1.rank_ref, s32[8,32]{1,0:T(8,128)S(1)} %copy-done, ...), custom_call_target="tpu_custom_call", output_to_operand_aliasing={{0}: (7, {}), {1}: (8, {}), {2}: (9, {}), {3}: (10, {})} | custom-call | flops 1 | bytes 1 | tf_op jit(solution)/shard_map/update_items/pallas_call | solution.py:285
  43.8 0.0 collective-permute-done.6.rest_0_
  43.8 1.3 %update_items.10 = (f32[1024,1024]{1,0:T(8,128)S(1)}, f32[1024,1024]{1,0:T(8,128)S(1)}, f32[1024,1024]{1,0:T(8,128)S(1)}, f32[1024,128]{1,0:T(8,128)S(1)}) custom-call(s32[1]{0:T(128)} %bitcast.1.rank_ref, s32[8,32]{1,0:T(8,128)S(1)} %copy-done, ...), custom_call_target="tpu_custom_call", output_to_operand_aliasing={{0}: (7, {}), {1}: (8, {}), {2}: (9, {}), {3}: (10, {})} | custom-call | flops 1 | bytes 1 | tf_op jit(solution)/shard_map/update_items/pallas_call | solution.py:285
  45.1 9.0 %collective-permute-done.5.rest_0_ = bf16[2,4,256,128]{3,2,1,0:T(8,128)(2,1)S(1)} collective-permute-done((bf16[2,4,256,128]{3,2,1,0:T(8,128)(2,1)S(1)}, bf16[2,4,256,128]{3,2,1,0:T(8,128)(2,1)S(1)}, u32[]{:S(2)}, u32[]{:S(2)}) %collective-permute-start.5) | collective-permute-done | bytes 524320 | tf_op jit(solution)/shard_map/match4/ppermute | solution.py:342
  54.1 1.3 %update_items.11 = (f32[1024,1024]{1,0:T(8,128)S(1)}, f32[1024,1024]{1,0:T(8,128)S(1)}, f32[1024,1024]{1,0:T(8,128)S(1)}, f32[1024,128]{1,0:T(8,128)S(1)}) custom-call(s32[1]{0:T(128)} %bitcast.1.rank_ref, s32[8,32]{1,0:T(8,128)S(1)} %copy-done, ...), custom_call_target="tpu_custom_call", output_to_operand_aliasing={{0}: (7, {}), {1}: (8, {}), {2}: (9, {}), {3}: (10, {})} | custom-call | flops 1 | bytes 1 | tf_op jit(solution)/shard_map/update_items/pallas_call | solution.py:285
  55.4 0.0 collective-permute-done.4.rest_0_
  55.4 1.3 %update_items.12 = (f32[1024,1024]{1,0:T(8,128)S(1)}, f32[1024,1024]{1,0:T(8,128)S(1)}, f32[1024,1024]{1,0:T(8,128)S(1)}, f32[1024,128]{1,0:T(8,128)S(1)}) custom-call(s32[1]{0:T(128)} %bitcast.1.rank_ref, s32[8,32]{1,0:T(8,128)S(1)} %copy-done, ...), custom_call_target="tpu_custom_call", output_to_operand_aliasing={{0}: (7, {}), {1}: (8, {}), {2}: (9, {}), {3}: (10, {})} | custom-call | flops 1 | bytes 1 | tf_op jit(solution)/shard_map/update_items/pallas_call | solution.py:285
  56.7 8.5 %collective-permute-done.1.rest_0_ = bf16[2,4,256,128]{3,2,1,0:T(8,128)(2,1)S(1)} collective-permute-done((bf16[2,4,256,128]{3,2,1,0:T(8,128)(2,1)S(1)}, bf16[2,4,256,128]{3,2,1,0:T(8,128)(2,1)S(1)}, u32[]{:S(2)}, u32[]{:S(2)}) %collective-permute-start.1) | collective-permute-done | bytes 524320 | tf_op jit(solution)/shard_map/match5/ppermute | solution.py:342
  65.2 1.1 %collective-permute-done.3.rest_1_ = bf16[2,4,256,128]{3,2,1,0:T(8,128)(2,1)S(1)} collective-permute-done((bf16[2,4,256,128]{3,2,1,0:T(8,128)(2,1)S(1)}, bf16[2,4,256,128]{3,2,1,0:T(8,128)(2,1)S(1)}, u32[]{:S(2)}, u32[]{:S(2)}) %collective-permute-start.3) | collective-permute-done | bytes 524320 | tf_op jit(solution)/shard_map/match3/ppermute | solution.py:342
  66.3 2.3 %update_items.13 = (f32[1024,1024]{1,0:T(8,128)S(1)}, f32[1024,1024]{1,0:T(8,128)S(1)}, f32[1024,1024]{1,0:T(8,128)S(1)}, f32[1024,128]{1,0:T(8,128)S(1)}, f32[1,1024]{1,0:T(1,128)S(1)}) custom-call(s32[1]{0:T(128)} %bitcast.1.rank_ref, s32[8,32]{1,0:T(8,128)S(1)} %copy-done, ...), custom_call_target="tpu_custom_call", output_to_operand_aliasing={{0}: (8, {}), {1}: (9, {}), {2}: (10, {}), {3}: (11, {})} | custom-call | flops 1 | bytes 1 | tf_op jit(solution)/shard_map/update_items/pallas_call | solution.py:285
  68.6 3.6 %collective-permute-start.10 = (f32[1,1024]{1,0:T(1,128)S(1)}, f32[1,1024]{1,0:T(1,128)S(1)}, u32[]{:S(2)}, u32[]{:S(2)}) collective-permute-start(f32[1,1024]{1,0:T(1,128)S(1)} %get-tuple-element.87.rest_0_), channel_id=1, source_target_pairs={{0,3},{1,2},{2,1},{3,0},{4,7},{5,6},{6,5},{7,4},{8,11},{9,10},{10,... | collective-permute-start | bytes 12296 | tf_op jit(solution)/shard_map/ppermute | solution.py:363
  72.2 0.0 collective-permute-start.9
  72.2 0.8 collective-permute-start.8
  73.0 1.0 %collective-permute-done.10.rest_3_ = f32[1,1024]{1,0:T(1,128)S(1)} collective-permute-done((f32[1,1024]{1,0:T(1,128)S(1)}, f32[1,1024]{1,0:T(1,128)S(1)}, u32[]{:S(2)}, u32[]{:S(2)}) %collective-permute-start.10) | collective-permute-done | bytes 4128 | tf_op jit(solution)/shard_map/ppermute | solution.py:363
  74.0 2.7 %collective-permute-done.9.rest_2_ = f32[1,1024]{1,0:T(1,128)S(1)} collective-permute-done((f32[1,1024]{1,0:T(1,128)S(1)}, f32[1,1024]{1,0:T(1,128)S(1)}, u32[]{:S(2)}, u32[]{:S(2)}) %collective-permute-start.9) | collective-permute-done | bytes 4128 | tf_op jit(solution)/shard_map/ppermute | solution.py:363
  76.7 0.0 collective-permute-done.8.rest_1_
  76.8 1.8 %scale_rows.1 = bf16[1024,1024]{1,0:T(8,128)(2,1)} custom-call(f32[1,1024]{1,0:T(1,128)S(1)} %bitcast.2, f32[1,1024]{1,0:T(1,128)S(1)} %get-tuple-element.87.rest_0_, f32[1,1024]{1,0:T(1,128)S(1)} %collective-permute-done.8.rest_1_, f32[1,1024]{1,0:T(1,128)S(1)} %collective-permute-done.9.rest_2_, f32[1,1024]{1,0:T(1,128)S(1)} %collective-permute-done.10.rest_3_, ...), custom_call_target="tpu_custom_call" | custom-call | tf_op jit(solution)/shard_map/scale_rows/pallas_call | solution.py:318
  (4 shorter events, 0.0 us)
Async XLA Ops:
  0.0 11.4 %copy-start = (s32[8,32]{1,0:T(8,128)S(1)}, s32[8,32]{1,0:T(8,128)}, u32[]{:S(2)}) copy-start(s32[8,32]{1,0:T(8,128)} %perm.15) | copy-start | bytes 3076
  2.8 19.4 %collective-permute-start = (bf16[2,256,1024]{2,1,0:T(8,128)(2,1)S(1)}, bf16[2,256,1024]{2,1,0:T(8,128)(2,1)S(1)}, u32[]{:S(2)}, u32[]{:S(2)}) collective-permute-start(bf16[2,256,1024]{2,1,0:T(8,128)(2,1)S(1)} %get-tuple-element.51), channel_id=1, source_target_pairs={{0,4},{4,8},{8,12},{12,16},{16,20},{20,24},{24,28},{1,5},{5,9},{9,... | collective-permute-start | bytes 3145736 | tf_op jit(solution)/shard_map/previous/ppermute | solution.py:348
  5.2 27.0 %collective-permute-start.2 = (bf16[2,4,256,128]{3,2,1,0:T(8,128)(2,1)S(1)}, bf16[2,4,256,128]{3,2,1,0:T(8,128)(2,1)S(1)}, u32[]{:S(2)}, u32[]{:S(2)}) collective-permute-start(bf16[2,4,256,128]{3,2,1,0:T(8,128)(2,1)S(1)} %get-tuple-element.57), channel_id=1, source_target_pairs={{0,4},{4,0},{8,12},{12,8},{16,20},{20,16},{24,28},{28,24},{1,5},{5... | collective-permute-start | bytes 1572872 | tf_op jit(solution)/shard_map/match1/ppermute | solution.py:342
  7.8 26.8 %collective-permute-start.7 = (bf16[2,4,256,128]{3,2,1,0:T(8,128)(2,1)S(1)}, bf16[2,4,256,128]{3,2,1,0:T(8,128)(2,1)S(1)}, u32[]{:S(2)}, u32[]{:S(2)}) collective-permute-start(bf16[2,4,256,128]{3,2,1,0:T(8,128)(2,1)S(1)} %get-tuple-element.66), channel_id=1, source_target_pairs={{0,24},{4,28},{8,16},{12,20},{16,8},{20,12},{24,0},{28,4},{1,25},{... | collective-permute-start | bytes 1572872 | tf_op jit(solution)/shard_map/match6/ppermute | solution.py:342
  8.8 45.3 %collective-permute-start.5 = (bf16[2,4,256,128]{3,2,1,0:T(8,128)(2,1)S(1)}, bf16[2,4,256,128]{3,2,1,0:T(8,128)(2,1)S(1)}, u32[]{:S(2)}, u32[]{:S(2)}) collective-permute-start(bf16[2,4,256,128]{3,2,1,0:T(8,128)(2,1)S(1)} %get-tuple-element.64), channel_id=1, source_target_pairs={{0,16},{4,20},{8,24},{12,28},{16,0},{20,4},{24,8},{28,12},{1,17},{... | collective-permute-start | bytes 1572872 | tf_op jit(solution)/shard_map/match4/ppermute | solution.py:342
  10.8 33.0 %collective-permute-start.6 = (bf16[2,4,256,128]{3,2,1,0:T(8,128)(2,1)S(1)}, bf16[2,4,256,128]{3,2,1,0:T(8,128)(2,1)S(1)}, u32[]{:S(2)}, u32[]{:S(2)}) collective-permute-start(bf16[2,4,256,128]{3,2,1,0:T(8,128)(2,1)S(1)} %get-tuple-element.65), channel_id=1, source_target_pairs={{0,28},{4,24},{8,20},{12,16},{16,12},{20,8},{24,4},{28,0},{1,29},{... | collective-permute-start | bytes 1572872 | tf_op jit(solution)/shard_map/match7/ppermute | solution.py:342
  22.2 33.2 %collective-permute-start.4 = (bf16[2,4,256,128]{3,2,1,0:T(8,128)(2,1)S(1)}, bf16[2,4,256,128]{3,2,1,0:T(8,128)(2,1)S(1)}, u32[]{:S(2)}, u32[]{:S(2)}) collective-permute-start(bf16[2,4,256,128]{3,2,1,0:T(8,128)(2,1)S(1)} %get-tuple-element.63), channel_id=1, source_target_pairs={{0,8},{4,12},{8,0},{12,4},{16,24},{20,28},{24,16},{28,20},{1,9},{5... | collective-permute-start | bytes 1572872 | tf_op jit(solution)/shard_map/match2/ppermute | solution.py:342
  32.2 33.0 %collective-permute-start.1 = (bf16[2,4,256,128]{3,2,1,0:T(8,128)(2,1)S(1)}, bf16[2,4,256,128]{3,2,1,0:T(8,128)(2,1)S(1)}, u32[]{:S(2)}, u32[]{:S(2)}) collective-permute-start(bf16[2,4,256,128]{3,2,1,0:T(8,128)(2,1)S(1)} %get-tuple-element.56), channel_id=1, source_target_pairs={{0,20},{4,16},{8,28},{12,24},{16,4},{20,0},{24,12},{28,8},{1,21},{... | collective-permute-start | bytes 1572872 | tf_op jit(solution)/shard_map/match5/ppermute | solution.py:342
  34.7 31.6 %collective-permute-start.3 = (bf16[2,4,256,128]{3,2,1,0:T(8,128)(2,1)S(1)}, bf16[2,4,256,128]{3,2,1,0:T(8,128)(2,1)S(1)}, u32[]{:S(2)}, u32[]{:S(2)}) collective-permute-start(bf16[2,4,256,128]{3,2,1,0:T(8,128)(2,1)S(1)} %get-tuple-element.62), channel_id=1, source_target_pairs={{0,12},{4,8},{8,4},{12,0},{16,28},{20,24},{24,20},{28,16},{1,13},{... | collective-permute-start | bytes 1572872 | tf_op jit(solution)/shard_map/match3/ppermute | solution.py:342
  66.3 10.5 %copy-start.1 = (f32[1024]{0:T(1024)S(1)}, f32[1024]{0:T(1024)}, u32[]{:S(2)}) copy-start(f32[1024]{0:T(1024)} %param.9) | copy-start | bytes 12292
  68.6 5.4 %collective-permute-start.10 = (f32[1,1024]{1,0:T(1,128)S(1)}, f32[1,1024]{1,0:T(1,128)S(1)}, u32[]{:S(2)}, u32[]{:S(2)}) collective-permute-start(f32[1,1024]{1,0:T(1,128)S(1)} %get-tuple-element.87.rest_0_), channel_id=1, source_target_pairs={{0,3},{1,2},{2,1},{3,0},{4,7},{5,6},{6,5},{7,4},{8,11},{9,10},{10,... | collective-permute-start | bytes 12296 | tf_op jit(solution)/shard_map/ppermute | solution.py:363
  72.2 4.5 %collective-permute-start.9 = (f32[1,1024]{1,0:T(1,128)S(1)}, f32[1,1024]{1,0:T(1,128)S(1)}, u32[]{:S(2)}, u32[]{:S(2)}) collective-permute-start(f32[1,1024]{1,0:T(1,128)S(1)} %get-tuple-element.87.rest_0_), channel_id=1, source_target_pairs={{0,2},{1,3},{2,0},{3,1},{4,6},{5,7},{6,4},{7,5},{8,10},{9,11},{10,... | collective-permute-start | bytes 12296 | tf_op jit(solution)/shard_map/ppermute | solution.py:363
  72.2 4.5 %collective-permute-start.8 = (f32[1,1024]{1,0:T(1,128)S(1)}, f32[1,1024]{1,0:T(1,128)S(1)}, u32[]{:S(2)}, u32[]{:S(2)}) collective-permute-start(f32[1,1024]{1,0:T(1,128)S(1)} %get-tuple-element.87.rest_0_), channel_id=1, source_target_pairs={{0,1},{1,0},{2,3},{3,2},{4,5},{5,4},{6,7},{7,6},{8,9},{9,8},{10,11... | collective-permute-start | bytes 12296 | tf_op jit(solution)/shard_map/ppermute | solution.py:363
where the time goes:
time: 78.9 us; the launch traced here: 78.7 us
  starting transfers between devices  30 us (38%)
  Pallas kernels  26.1 us (33%)
  waiting for transfers between devices  22.4 us (28%)
    ppermute x7, starting transfers between devices, exchange(): received[d] = lax.ppermute(array, 'ctx', route)  23.1 us
    ppermute x7, waiting for transfers between devices, exchange(): received[d] = lax.ppermute(array, 'ctx', route)  18.6 us
    pallas_call x1, Pallas kernels, base(): pl.pallas_call(functools.partial(base_kernel, sizes, partners), out_shape...  10.8 us
    pallas_call x7, Pallas kernels, update(): pl.pallas_call(functools.partial(update_kernel, sizes, group, partners, l...  10.7 us
    ppermute x3, starting transfers between devices, per_device(): lax.ppermute(sums[0], 'head', [(i, i ^ d) for i in range(head_size)])  4.42 us
    ppermute x3, waiting for transfers between devices, per_device(): lax.ppermute(sums[0], 'head', [(i, i ^ d) for i in range(head_size)])  3.72 us
    pallas_call x1, Pallas kernels, first_sends(): pl.pallas_call(functools.partial(first_kernel, sizes, partners), out_shap...  2.78 us
    ppermute x1, starting transfers between devices, per_device(): received['prev'] = lax.ppermute(last_block, 'ctx', route)  2.42 us
  transfers between devices with their start and end apart: 11, of which 5 were waited for; matrix products, arithmetic and copies ran while one was open for 0% of the time, Pallas kernels for 24%

commit v1 on v0

--- a/solution.py
+++ b/solution.py
@@ -78,8 +78,33 @@
         pack_near(sizes, items, which, array, send)
 
 
+def last_kernel(block_len, keys, values, last, sems):
+    rows = pl.ds(keys.shape[0] - block_len, block_len)
+    copies = [
+        pltpu.make_async_copy(array.at[rows], last.at[i], sems.at[i])
+        for i, array in enumerate((keys, values))
+    ]
+    for copy in copies:
+        copy.start()
+    for copy in copies:
+        copy.wait()
+
+
+def last_blocks(sizes, keys, values):
+    return pl.pallas_call(
+        functools.partial(last_kernel, sizes.block_len),
+        out_shape=pltpu.VMEM((2, sizes.block_len, sizes.width), keys.dtype),
+        in_specs=[ANY, ANY],
+        out_specs=VMEM,
+        scratch_shapes=[pltpu.SemaphoreType.DMA((2,))],
+        compiler_params=PARAMS,
+        cost_estimate=pl.CostEstimate(flops=1, bytes_accessed=1, transcendentals=0),
+        name="last_blocks",
+    )(far(keys), far(values))
+
+
 def first_kernel(
-    sizes, partners, rank_ref, perm_far, keys, values, near_keys, near_values, last, *rest
+    sizes, partners, rank_ref, perm_far, keys, values, near_keys, near_values, *rest
 ):
     sends, (perm, perm_sem, sems) = rest[:-3], rest[-3:]
     perm_copy = pltpu.make_async_copy(perm_far, perm, perm_sem.at[0])
@@ -94,19 +119,17 @@
     found = [list(wanted(sizes, d, rank_ref[0], perm)) for d in partners]
     for i, (copy, array) in enumerate(zip(copies, (near_keys, near_values))):
         copy.wait()
-        last[i] = array[sizes.tokens - sizes.block_len :]
         for items, send in zip(found, sends):
             pack_near(sizes, items, i, array, send)
 
 
 def first_sends(sizes, partners, rank, perm, keys, values):
-    near_keys, near_values, last, *sends = pl.pallas_call(
+    near_keys, near_values, *sends = pl.pallas_call(
         functools.partial(first_kernel, sizes, partners),
         out_shape=[pltpu.VMEM(keys.shape, keys.dtype)] * 2
-        + [pltpu.VMEM((2, sizes.block_len, sizes.width), keys.dtype)]
         + [pltpu.VMEM(sizes.send_shape(), keys.dtype)] * len(partners),
         in_specs=[SMEM, ANY, ANY, ANY],
-        out_specs=[VMEM] * (3 + len(partners)),
+        out_specs=[VMEM] * (2 + len(partners)),
         scratch_shapes=[
             pltpu.SMEM(perm.shape, perm.dtype),
             pltpu.SemaphoreType.DMA((1,)),
@@ -116,7 +139,7 @@
         cost_estimate=pl.CostEstimate(flops=1, bytes_accessed=1, transcendentals=0),
         name="first_sends",
     )(rank, far(perm), far(keys), far(values))
-    return near_keys, near_values, last, dict(zip(partners, sends))
+    return near_keys, near_values, dict(zip(partners, sends))
 
 
 def weigh(sizes, scores, peak, values):
@@ -342,7 +365,8 @@
                 received[d] = lax.ppermute(array, "ctx", route)
 
     first, steps = schedule(sizes.ctx)
-    keys, values, last_block, sends = first_sends(sizes, first, rank, block_perm, keys, values)
+    last_block = last_blocks(sizes, keys, values)
+    keys, values, sends = first_sends(sizes, first, rank, block_perm, keys, values)
     with jax.named_scope("previous"):
         route = [(i, i + 1) for i in range(sizes.ctx - 1)]
         received["prev"] = lax.ppermute(last_block, "ctx", route)

time: 78.9 us -> 77.3 us (0.980)
  starting transfers between devices: 30 us -> 24.5 us
  waiting for transfers between devices: 22.4 us -> 25.1 us
  Pallas kernels: 26.1 us -> 27.2 us
    ppermute x7, starting transfers between devices: 23.1 us -> 17.6 us  [exchange(): received[d] = lax.ppermute(array, 'ctx', route)]
    ppermute x7, waiting for transfers between devices: 18.6 us -> 21.4 us  [exchange(): received[d] = lax.ppermute(array, 'ctx', route)]
    pallas_call x0 -> x1, Pallas kernels: none -> 1.23 us  [last_blocks(): pl.pallas_call(functools.partial(last_kernel, sizes.block_len), out_shape...]
  transfers between devices with their start and end apart: 11 -> 11, of which waited for: 5 -> 5; matrix products, arithmetic and copies ran while one was open for 0% -> 0% of each run, Pallas kernels for 24% -> 28%
where the time goes in v1:
time: 77.3 us; the launch traced here: 77.1 us
  Pallas kernels  27.2 us (35%)
  waiting for transfers between devices  25.1 us (32%)
  starting transfers between devices  24.5 us (32%)
    ppermute x7, waiting for transfers between devices, exchange(): received[d] = lax.ppermute(array, 'ctx', route)  21.4 us
    ppermute x7, starting transfers between devices, exchange(): received[d] = lax.ppermute(array, 'ctx', route)  17.6 us
    pallas_call x1, Pallas kernels, base(): pl.pallas_call(functools.partial(base_kernel, sizes, partners), out_shape...  10.8 us
    pallas_call x7, Pallas kernels, update(): pl.pallas_call(functools.partial(update_kernel, sizes, group, partners, l...  10.7 us
    ppermute x3, starting transfers between devices, per_device(): lax.ppermute(sums[0], 'head', [(i, i ^ d) for i in range(head_size)])  4.42 us
    ppermute x3, waiting for transfers between devices, per_device(): lax.ppermute(sums[0], 'head', [(i, i ^ d) for i in range(head_size)])  3.72 us
    pallas_call x1, Pallas kernels, first_sends(): pl.pallas_call(functools.partial(first_kernel, sizes, partners), out_shap...  2.73 us
    ppermute x1, starting transfers between devices, per_device(): received['prev'] = lax.ppermute(last_block, 'ctx', route)  2.42 us
  transfers between devices with their start and end apart: 11, of which 5 were waited for; matrix products, arithmetic and copies ran while one was open for 0% of the time, Pallas kernels for 28%

profile of v1, /device:TPU:0, one launch (start us, length us, event | category | flops | bytes accessed | tf_op | source)
XLA Modules:
  0.0 77.1 jit_solution(4645160834033377063)
XLA Ops:
  0.0 1.2 %last_blocks.1 = bf16[2,256,1024]{2,1,0:T(8,128)(2,1)S(1)} custom-call(bf16[1024,1024]{1,0:T(8,128)(2,1)} %keys.3, bf16[1024,1024]{1,0:T(8,128)(2,1)} %values.3), custom_call_target="tpu_custom_call" | custom-call | flops 1 | bytes 1 | tf_op jit(solution)/shard_map/last_blocks/pallas_call | solution.py:94
  1.2 2.4 %collective-permute-start = (bf16[2,256,1024]{2,1,0:T(8,128)(2,1)S(1)}, bf16[2,256,1024]{2,1,0:T(8,128)(2,1)S(1)}, u32[]{:S(2)}, u32[]{:S(2)}) collective-permute-start(bf16[2,256,1024]{2,1,0:T(8,128)(2,1)S(1)} %last_blocks.1), channel_id=1, source_target_pairs={{0,4},{4,8},{8,12},{12,16},{16,20},{20,24},{24,28},{1,5},{5,9},{9,... | collective-permute-start | bytes 3145736 | tf_op jit(solution)/shard_map/previous/ppermute | solution.py:372
  3.7 2.7 %first_sends.1 = (bf16[1024,1024]{1,0:T(8,128)(2,1)S(1)}, bf16[1024,1024]{1,0:T(8,128)(2,1)S(1)}, bf16[2,4,256,128]{3,2,1,0:T(8,128)(2,1)S(1)}, bf16[2,4,256,128...) custom-call(s32[1]{0:T(128)} %bitcast.1.rank_ref, s32[8,32]{1,0:T(8,128)} %perm.15, ...), custom_call_target="tpu_custom_call" | custom-call | flops 1 | bytes 1 | tf_op jit(solution)/shard_map/first_sends/pallas_call | solution.py:127
  6.4 2.6 %collective-permute-start.2 = (bf16[2,4,256,128]{3,2,1,0:T(8,128)(2,1)S(1)}, bf16[2,4,256,128]{3,2,1,0:T(8,128)(2,1)S(1)}, u32[]{:S(2)}, u32[]{:S(2)}) collective-permute-start(bf16[2,4,256,128]{3,2,1,0:T(8,128)(2,1)S(1)} %get-tuple-element.55), channel_id=1, source_target_pairs={{0,4},{4,0},{8,12},{12,8},{16,20},{20,16},{24,28},{28,24},{1,5},{5... | collective-permute-start | bytes 1572872 | tf_op jit(solution)/shard_map/match1/ppermute | solution.py:365
  9.0 0.9 %collective-permute-start.7 = (bf16[2,4,256,128]{3,2,1,0:T(8,128)(2,1)S(1)}, bf16[2,4,256,128]{3,2,1,0:T(8,128)(2,1)S(1)}, u32[]{:S(2)}, u32[]{:S(2)}) collective-permute-start(bf16[2,4,256,128]{3,2,1,0:T(8,128)(2,1)S(1)} %get-tuple-element.64), channel_id=1, source_target_pairs={{0,24},{4,28},{8,16},{12,20},{16,8},{20,12},{24,0},{28,4},{1,25},{... | collective-permute-start | bytes 1572872 | tf_op jit(solution)/shard_map/match6/ppermute | solution.py:365
  10.0 2.0 %collective-permute-start.5 = (bf16[2,4,256,128]{3,2,1,0:T(8,128)(2,1)S(1)}, bf16[2,4,256,128]{3,2,1,0:T(8,128)(2,1)S(1)}, u32[]{:S(2)}, u32[]{:S(2)}) collective-permute-start(bf16[2,4,256,128]{3,2,1,0:T(8,128)(2,1)S(1)} %get-tuple-element.62), channel_id=1, source_target_pairs={{0,16},{4,20},{8,24},{12,28},{16,0},{20,4},{24,8},{28,12},{1,17},{... | collective-permute-start | bytes 1572872 | tf_op jit(solution)/shard_map/match4/ppermute | solution.py:365
  12.0 0.6 collective-permute-start.6
  12.6 10.8 %base_items.1 = (bf16[1024,1024]{1,0:T(8,128)(2,1)S(1)}, f32[1024,1024]{1,0:T(8,128)S(1)}, f32[1024,1024]{1,0:T(8,128)S(1)}, f32[1024,1024]{1,0:T(8,128)S(1)}, f...) custom-call(s32[1]{0:T(128)} %bitcast.1.rank_ref, s32[8,32]{1,0:T(8,128)S(1)} %copy-done, ...), custom_call_target="tpu_custom_call" | custom-call | flops 1 | bytes 1 | tf_op jit(solution)/shard_map/base_items/pallas_call | solution.py:210
  23.4 0.0 collective-permute-done.rest_0_
  23.4 3.6 %collective-permute-start.4 = (bf16[2,4,256,128]{3,2,1,0:T(8,128)(2,1)S(1)}, bf16[2,4,256,128]{3,2,1,0:T(8,128)(2,1)S(1)}, u32[]{:S(2)}, u32[]{:S(2)}) collective-permute-start(bf16[2,4,256,128]{3,2,1,0:T(8,128)(2,1)S(1)} %get-tuple-element.61), channel_id=1, source_target_pairs={{0,8},{4,12},{8,0},{12,4},{16,24},{20,28},{24,16},{28,20},{1,9},{5... | collective-permute-start | bytes 1572872 | tf_op jit(solution)/shard_map/match2/ppermute | solution.py:365
  27.0 0.9 %update_items.7 = (f32[1024,1024]{1,0:T(8,128)S(1)}, f32[1024,1024]{1,0:T(8,128)S(1)}, f32[1024,1024]{1,0:T(8,128)S(1)}, f32[1024,128]{1,0:T(8,128)S(1)}, bf16[2,4,256,128]{3,2,1,0:T(8,128)(2,1)S(1)}) custom-call(s32[1]{0:T(128)} %bitcast.1.rank_ref, s32[8,32]{1,0:T(8,128)S(1)} %copy-done, ...), custom_call_target="tpu_custom_call", output_to_operand_aliasing={{0}: (7, {}), {1}: (8, {}), {2}: (9, {}), {3}: (10, {})} | custom-call | flops 1 | bytes 1 | tf_op jit(solution)/shard_map/update_items/pallas_call | solution.py:308
  27.9 0.0 collective-permute-done.2.rest_0_
  27.9 0.1 collective-permute-start.1
  28.0 2.3 %update_items.8 = (f32[1024,1024]{1,0:T(8,128)S(1)}, f32[1024,1024]{1,0:T(8,128)S(1)}, f32[1024,1024]{1,0:T(8,128)S(1)}, f32[1024,128]{1,0:T(8,128)S(1)}, bf16[2,4,256,128]{3,2,1,0:T(8,128)(2,1)S(1)}) custom-call(s32[1]{0:T(128)} %bitcast.1.rank_ref, s32[8,32]{1,0:T(8,128)S(1)} %copy-done, ...), custom_call_target="tpu_custom_call", output_to_operand_aliasing={{0}: (7, {}), {1}: (8, {}), {2}: (9, {}), {3}: (10, {})} | custom-call | flops 1 | bytes 1 | tf_op jit(solution)/shard_map/update_items/pallas_call | solution.py:308
  30.3 0.0 collective-permute-done.7.rest_0_
  30.3 7.8 %collective-permute-start.3 = (bf16[2,4,256,128]{3,2,1,0:T(8,128)(2,1)S(1)}, bf16[2,4,256,128]{3,2,1,0:T(8,128)(2,1)S(1)}, u32[]{:S(2)}, u32[]{:S(2)}) collective-permute-start(bf16[2,4,256,128]{3,2,1,0:T(8,128)(2,1)S(1)} %get-tuple-element.60), channel_id=1, source_target_pairs={{0,12},{4,8},{8,4},{12,0},{16,28},{20,24},{24,20},{28,16},{1,13},{... | collective-permute-start | bytes 1572872 | tf_op jit(solution)/shard_map/match3/ppermute | solution.py:365
  38.2 1.3 %update_items.9 = (f32[1024,1024]{1,0:T(8,128)S(1)}, f32[1024,1024]{1,0:T(8,128)S(1)}, f32[1024,1024]{1,0:T(8,128)S(1)}, f32[1024,128]{1,0:T(8,128)S(1)}) custom-call(s32[1]{0:T(128)} %bitcast.1.rank_ref, s32[8,32]{1,0:T(8,128)S(1)} %copy-done, ...), custom_call_target="tpu_custom_call", output_to_operand_aliasing={{0}: (7, {}), {1}: (8, {}), {2}: (9, {}), {3}: (10, {})} | custom-call | flops 1 | bytes 1 | tf_op jit(solution)/shard_map/update_items/pallas_call | solution.py:308
  39.5 0.0 collective-permute-done.6.rest_0_
  39.5 1.3 %update_items.10 = (f32[1024,1024]{1,0:T(8,128)S(1)}, f32[1024,1024]{1,0:T(8,128)S(1)}, f32[1024,1024]{1,0:T(8,128)S(1)}, f32[1024,128]{1,0:T(8,128)S(1)}) custom-call(s32[1]{0:T(128)} %bitcast.1.rank_ref, s32[8,32]{1,0:T(8,128)S(1)} %copy-done, ...), custom_call_target="tpu_custom_call", output_to_operand_aliasing={{0}: (7, {}), {1}: (8, {}), {2}: (9, {}), {3}: (10, {})} | custom-call | flops 1 | bytes 1 | tf_op jit(solution)/shard_map/update_items/pallas_call | solution.py:308
  40.8 11.8 %collective-permute-done.5.rest_0_ = bf16[2,4,256,128]{3,2,1,0:T(8,128)(2,1)S(1)} collective-permute-done((bf16[2,4,256,128]{3,2,1,0:T(8,128)(2,1)S(1)}, bf16[2,4,256,128]{3,2,1,0:T(8,128)(2,1)S(1)}, u32[]{:S(2)}, u32[]{:S(2)}) %collective-permute-start.5) | collective-permute-done | bytes 524320 | tf_op jit(solution)/shard_map/match4/ppermute | solution.py:365
  52.5 1.3 %update_items.11 = (f32[1024,1024]{1,0:T(8,128)S(1)}, f32[1024,1024]{1,0:T(8,128)S(1)}, f32[1024,1024]{1,0:T(8,128)S(1)}, f32[1024,128]{1,0:T(8,128)S(1)}) custom-call(s32[1]{0:T(128)} %bitcast.1.rank_ref, s32[8,32]{1,0:T(8,128)S(1)} %copy-done, ...), custom_call_target="tpu_custom_call", output_to_operand_aliasing={{0}: (7, {}), {1}: (8, {}), {2}: (9, {}), {3}: (10, {})} | custom-call | flops 1 | bytes 1 | tf_op jit(solution)/shard_map/update_items/pallas_call | solution.py:308
  53.8 0.0 collective-permute-done.4.rest_0_
  53.8 1.3 %update_items.12 = (f32[1024,1024]{1,0:T(8,128)S(1)}, f32[1024,1024]{1,0:T(8,128)S(1)}, f32[1024,1024]{1,0:T(8,128)S(1)}, f32[1024,128]{1,0:T(8,128)S(1)}) custom-call(s32[1]{0:T(128)} %bitcast.1.rank_ref, s32[8,32]{1,0:T(8,128)S(1)} %copy-done, ...), custom_call_target="tpu_custom_call", output_to_operand_aliasing={{0}: (7, {}), {1}: (8, {}), {2}: (9, {}), {3}: (10, {})} | custom-call | flops 1 | bytes 1 | tf_op jit(solution)/shard_map/update_items/pallas_call | solution.py:308
  55.1 8.5 %collective-permute-done.1.rest_0_ = bf16[2,4,256,128]{3,2,1,0:T(8,128)(2,1)S(1)} collective-permute-done((bf16[2,4,256,128]{3,2,1,0:T(8,128)(2,1)S(1)}, bf16[2,4,256,128]{3,2,1,0:T(8,128)(2,1)S(1)}, u32[]{:S(2)}, u32[]{:S(2)}) %collective-permute-start.1) | collective-permute-done | bytes 524320 | tf_op jit(solution)/shard_map/match5/ppermute | solution.py:365
  63.7 1.1 %collective-permute-done.3.rest_1_ = bf16[2,4,256,128]{3,2,1,0:T(8,128)(2,1)S(1)} collective-permute-done((bf16[2,4,256,128]{3,2,1,0:T(8,128)(2,1)S(1)}, bf16[2,4,256,128]{3,2,1,0:T(8,128)(2,1)S(1)}, u32[]{:S(2)}, u32[]{:S(2)}) %collective-permute-start.3) | collective-permute-done | bytes 524320 | tf_op jit(solution)/shard_map/match3/ppermute | solution.py:365
  64.7 2.3 %update_items.13 = (f32[1024,1024]{1,0:T(8,128)S(1)}, f32[1024,1024]{1,0:T(8,128)S(1)}, f32[1024,1024]{1,0:T(8,128)S(1)}, f32[1024,128]{1,0:T(8,128)S(1)}, f32[1,1024]{1,0:T(1,128)S(1)}) custom-call(s32[1]{0:T(128)} %bitcast.1.rank_ref, s32[8,32]{1,0:T(8,128)S(1)} %copy-done, ...), custom_call_target="tpu_custom_call", output_to_operand_aliasing={{0}: (8, {}), {1}: (9, {}), {2}: (10, {}), {3}: (11, {})} | custom-call | flops 1 | bytes 1 | tf_op jit(solution)/shard_map/update_items/pallas_call | solution.py:308
  67.1 3.6 %collective-permute-start.10 = (f32[1,1024]{1,0:T(1,128)S(1)}, f32[1,1024]{1,0:T(1,128)S(1)}, u32[]{:S(2)}, u32[]{:S(2)}) collective-permute-start(f32[1,1024]{1,0:T(1,128)S(1)} %get-tuple-element.85.rest_0_), channel_id=1, source_target_pairs={{0,3},{1,2},{2,1},{3,0},{4,7},{5,6},{6,5},{7,4},{8,11},{9,10},{10,... | collective-permute-start | bytes 12296 | tf_op jit(solution)/shard_map/ppermute | solution.py:387
  70.7 0.0 collective-permute-start.9
  70.7 0.8 %collective-permute-start.8 = (f32[1,1024]{1,0:T(1,128)S(1)}, f32[1,1024]{1,0:T(1,128)S(1)}, u32[]{:S(2)}, u32[]{:S(2)}) collective-permute-start(f32[1,1024]{1,0:T(1,128)S(1)} %get-tuple-element.85.rest_0_), channel_id=1, source_target_pairs={{0,1},{1,0},{2,3},{3,2},{4,5},{5,4},{6,7},{7,6},{8,9},{9,8},{10,11... | collective-permute-start | bytes 12296 | tf_op jit(solution)/shard_map/ppermute | solution.py:387
  71.5 1.0 %collective-permute-done.10.rest_3_ = f32[1,1024]{1,0:T(1,128)S(1)} collective-permute-done((f32[1,1024]{1,0:T(1,128)S(1)}, f32[1,1024]{1,0:T(1,128)S(1)}, u32[]{:S(2)}, u32[]{:S(2)}) %collective-permute-start.10) | collective-permute-done | bytes 4128 | tf_op jit(solution)/shard_map/ppermute | solution.py:387
  72.5 2.7 %collective-permute-done.9.rest_2_ = f32[1,1024]{1,0:T(1,128)S(1)} collective-permute-done((f32[1,1024]{1,0:T(1,128)S(1)}, f32[1,1024]{1,0:T(1,128)S(1)}, u32[]{:S(2)}, u32[]{:S(2)}) %collective-permute-start.9) | collective-permute-done | bytes 4128 | tf_op jit(solution)/shard_map/ppermute | solution.py:387
  75.2 1.8 %scale_rows.1 = bf16[1024,1024]{1,0:T(8,128)(2,1)} custom-call(f32[1,1024]{1,0:T(1,128)S(1)} %bitcast.2, f32[1,1024]{1,0:T(1,128)S(1)} %get-tuple-element.85.rest_0_, f32[1,1024]{1,0:T(1,128)S(1)} %collective-permute-done.8.rest_1_, f32[1,1024]{1,0:T(1,128)S(1)} %collective-permute-done.9.rest_2_, f32[1,1024]{1,0:T(1,128)S(1)} %collective-permute-done.10.rest_3_, ...), custom_call_target="tpu_custom_call" | custom-call | tf_op jit(solution)/shard_map/scale_rows/pallas_call | solution.py:341
  (5 shorter events, 0.0 us)
Async XLA Ops:
  0.0 12.6 %copy-start = (s32[8,32]{1,0:T(8,128)S(1)}, s32[8,32]{1,0:T(8,128)}, u32[]{:S(2)}) copy-start(s32[8,32]{1,0:T(8,128)} %perm.15) | copy-start | bytes 3076
  1.2 22.2 %collective-permute-start = (bf16[2,256,1024]{2,1,0:T(8,128)(2,1)S(1)}, bf16[2,256,1024]{2,1,0:T(8,128)(2,1)S(1)}, u32[]{:S(2)}, u32[]{:S(2)}) collective-permute-start(bf16[2,256,1024]{2,1,0:T(8,128)(2,1)S(1)} %last_blocks.1), channel_id=1, source_target_pairs={{0,4},{4,8},{8,12},{12,16},{16,20},{20,24},{24,28},{1,5},{5,9},{9,... | collective-permute-start | bytes 3145736 | tf_op jit(solution)/shard_map/previous/ppermute | solution.py:372
  6.4 21.5 %collective-permute-start.2 = (bf16[2,4,256,128]{3,2,1,0:T(8,128)(2,1)S(1)}, bf16[2,4,256,128]{3,2,1,0:T(8,128)(2,1)S(1)}, u32[]{:S(2)}, u32[]{:S(2)}) collective-permute-start(bf16[2,4,256,128]{3,2,1,0:T(8,128)(2,1)S(1)} %get-tuple-element.55), channel_id=1, source_target_pairs={{0,4},{4,0},{8,12},{12,8},{16,20},{20,16},{24,28},{28,24},{1,5},{5... | collective-permute-start | bytes 1572872 | tf_op jit(solution)/shard_map/match1/ppermute | solution.py:365
  9.0 21.3 %collective-permute-start.7 = (bf16[2,4,256,128]{3,2,1,0:T(8,128)(2,1)S(1)}, bf16[2,4,256,128]{3,2,1,0:T(8,128)(2,1)S(1)}, u32[]{:S(2)}, u32[]{:S(2)}) collective-permute-start(bf16[2,4,256,128]{3,2,1,0:T(8,128)(2,1)S(1)} %get-tuple-element.64), channel_id=1, source_target_pairs={{0,24},{4,28},{8,16},{12,20},{16,8},{20,12},{24,0},{28,4},{1,25},{... | collective-permute-start | bytes 1572872 | tf_op jit(solution)/shard_map/match6/ppermute | solution.py:365
  10.0 42.6 %collective-permute-start.5 = (bf16[2,4,256,128]{3,2,1,0:T(8,128)(2,1)S(1)}, bf16[2,4,256,128]{3,2,1,0:T(8,128)(2,1)S(1)}, u32[]{:S(2)}, u32[]{:S(2)}) collective-permute-start(bf16[2,4,256,128]{3,2,1,0:T(8,128)(2,1)S(1)} %get-tuple-element.62), channel_id=1, source_target_pairs={{0,16},{4,20},{8,24},{12,28},{16,0},{20,4},{24,8},{28,12},{1,17},{... | collective-permute-start | bytes 1572872 | tf_op jit(solution)/shard_map/match4/ppermute | solution.py:365
  12.0 27.5 %collective-permute-start.6 = (bf16[2,4,256,128]{3,2,1,0:T(8,128)(2,1)S(1)}, bf16[2,4,256,128]{3,2,1,0:T(8,128)(2,1)S(1)}, u32[]{:S(2)}, u32[]{:S(2)}) collective-permute-start(bf16[2,4,256,128]{3,2,1,0:T(8,128)(2,1)S(1)} %get-tuple-element.63), channel_id=1, source_target_pairs={{0,28},{4,24},{8,20},{12,16},{16,12},{20,8},{24,4},{28,0},{1,29},{... | collective-permute-start | bytes 1572872 | tf_op jit(solution)/shard_map/match7/ppermute | solution.py:365
  23.4 30.4 %collective-permute-start.4 = (bf16[2,4,256,128]{3,2,1,0:T(8,128)(2,1)S(1)}, bf16[2,4,256,128]{3,2,1,0:T(8,128)(2,1)S(1)}, u32[]{:S(2)}, u32[]{:S(2)}) collective-permute-start(bf16[2,4,256,128]{3,2,1,0:T(8,128)(2,1)S(1)} %get-tuple-element.61), channel_id=1, source_target_pairs={{0,8},{4,12},{8,0},{12,4},{16,24},{20,28},{24,16},{28,20},{1,9},{5... | collective-permute-start | bytes 1572872 | tf_op jit(solution)/shard_map/match2/ppermute | solution.py:365
  27.9 35.8 %collective-permute-start.1 = (bf16[2,4,256,128]{3,2,1,0:T(8,128)(2,1)S(1)}, bf16[2,4,256,128]{3,2,1,0:T(8,128)(2,1)S(1)}, u32[]{:S(2)}, u32[]{:S(2)}) collective-permute-start(bf16[2,4,256,128]{3,2,1,0:T(8,128)(2,1)S(1)} %get-tuple-element.54), channel_id=1, source_target_pairs={{0,20},{4,16},{8,28},{12,24},{16,4},{20,0},{24,12},{28,8},{1,21},{... | collective-permute-start | bytes 1572872 | tf_op jit(solution)/shard_map/match5/ppermute | solution.py:365
  30.3 34.4 %collective-permute-start.3 = (bf16[2,4,256,128]{3,2,1,0:T(8,128)(2,1)S(1)}, bf16[2,4,256,128]{3,2,1,0:T(8,128)(2,1)S(1)}, u32[]{:S(2)}, u32[]{:S(2)}) collective-permute-start(bf16[2,4,256,128]{3,2,1,0:T(8,128)(2,1)S(1)} %get-tuple-element.60), channel_id=1, source_target_pairs={{0,12},{4,8},{8,4},{12,0},{16,28},{20,24},{24,20},{28,16},{1,13},{... | collective-permute-start | bytes 1572872 | tf_op jit(solution)/shard_map/match3/ppermute | solution.py:365
  64.7 10.4 %copy-start.1 = (f32[1024]{0:T(1024)S(1)}, f32[1024]{0:T(1024)}, u32[]{:S(2)}) copy-start(f32[1024]{0:T(1024)} %param.9) | copy-start | bytes 12292
  67.1 5.4 %collective-permute-start.10 = (f32[1,1024]{1,0:T(1,128)S(1)}, f32[1,1024]{1,0:T(1,128)S(1)}, u32[]{:S(2)}, u32[]{:S(2)}) collective-permute-start(f32[1,1024]{1,0:T(1,128)S(1)} %get-tuple-element.85.rest_0_), channel_id=1, source_target_pairs={{0,3},{1,2},{2,1},{3,0},{4,7},{5,6},{6,5},{7,4},{8,11},{9,10},{10,... | collective-permute-start | bytes 12296 | tf_op jit(solution)/shard_map/ppermute | solution.py:387
  70.7 4.5 %collective-permute-start.9 = (f32[1,1024]{1,0:T(1,128)S(1)}, f32[1,1024]{1,0:T(1,128)S(1)}, u32[]{:S(2)}, u32[]{:S(2)}) collective-permute-start(f32[1,1024]{1,0:T(1,128)S(1)} %get-tuple-element.85.rest_0_), channel_id=1, source_target_pairs={{0,2},{1,3},{2,0},{3,1},{4,6},{5,7},{6,4},{7,5},{8,10},{9,11},{10,... | collective-permute-start | bytes 12296 | tf_op jit(solution)/shard_map/ppermute | solution.py:387
  70.7 4.5 %collective-permute-start.8 = (f32[1,1024]{1,0:T(1,128)S(1)}, f32[1,1024]{1,0:T(1,128)S(1)}, u32[]{:S(2)}, u32[]{:S(2)}) collective-permute-start(f32[1,1024]{1,0:T(1,128)S(1)} %get-tuple-element.85.rest_0_), channel_id=1, source_target_pairs={{0,1},{1,0},{2,3},{3,2},{4,5},{5,4},{6,7},{7,6},{8,9},{9,8},{10,11... | collective-permute-start | bytes 12296 | tf_op jit(solution)/shard_map/ppermute | solution.py:387

commit v2 on v1

--- a/solution.py
+++ b/solution.py
@@ -32,16 +32,33 @@
         rows = pl.ds(pl.multiple_of(block * self.block_len, self.block_len), self.block_len)
         return rows, pl.ds(pl.multiple_of(head * self.head_dim, self.head_dim), self.head_dim)
 
-    def send_shape(self):
-        return (2, self.capacity, self.block_len, self.head_dim)
-
-
-def schedule(ctx):
+    def send_shape(self, message):
+        _, low, high = message
+        return (2, high - low, self.block_len, self.head_dim)
+
+
+def schedule(ctx, capacity):
+    whole = {d: (d, 0, capacity) for d in range(ctx)}
     if ctx == 8:
-        steps = [("base", [2]), ("prev", [5]), ((0, 1), [3])]
-        return [6, 7, 4, 1], steps + [((d,), []) for d in (6, 7, 4, 2)] + [((5, 3), [])]
-    rest = list(range(1, ctx))
-    return rest, [("base", []), ("prev", []), ((0,), [])] + [((d,), []) for d in rest]
+        half = capacity // 2
+        (five, last_five), (three, last_three) = [
+            ((d, 0, half), (d, half, capacity)) for d in (5, 3)
+        ]
+        steps = [
+            ("base", [whole[2]]),
+            ("prev", [five]),
+            ((whole[0], whole[1]), [three]),
+            ((whole[6],), [last_five]),
+            ((whole[7],), [last_three]),
+            ((whole[4],), []),
+            ((whole[2],), []),
+            ((five,), []),
+            ((three,), []),
+            ((last_five, last_three), []),
+        ]
+        return [whole[d] for d in (6, 7, 4, 1)], steps
+    rest = [whole[d] for d in range(1, ctx)]
+    return rest, [("base", []), ("prev", []), ((whole[0],), [])] + [((m,), []) for m in rest]
 
 
 def near(array):
@@ -64,18 +81,20 @@
         slot = slot + (found >= 0).astype(jnp.int32)
 
 
-def pack_near(sizes, items, which, array, send):
+def pack_near(sizes, message, items, which, array, send):
+    _, low, high = message
     for head, found, slot in items:
-
-        @pl.when(found >= 0)
+        here = (found >= 0) & (slot >= low) & (slot < high)
+
+        @pl.when(found >= 0 if high - low == sizes.capacity else here)
         def _():
-            send[which, slot] = array[sizes.tile(found, head)]
-
-
-def pack_both(sizes, d, rank, perm, keys, values, send):
-    items = list(wanted(sizes, d, rank, perm))
+            send[which, slot - low] = array[sizes.tile(found, head)]
+
+
+def pack_both(sizes, message, rank, perm, keys, values, send):
+    items = list(wanted(sizes, message[0], rank, perm))
     for which, array in enumerate((keys, values)):
-        pack_near(sizes, items, which, array, send)
+        pack_near(sizes, message, items, which, array, send)
 
 
 def last_kernel(block_len, keys, values, last, sems):
@@ -116,18 +135,18 @@
     for copy in copies:
         copy.start()
     perm_copy.wait()
-    found = [list(wanted(sizes, d, rank_ref[0], perm)) for d in partners]
+    found = [list(wanted(sizes, m[0], rank_ref[0], perm)) for m in partners]
     for i, (copy, array) in enumerate(zip(copies, (near_keys, near_values))):
         copy.wait()
-        for items, send in zip(found, sends):
-            pack_near(sizes, items, i, array, send)
+        for message, items, send in zip(partners, found, sends):
+            pack_near(sizes, message, items, i, array, send)
 
 
 def first_sends(sizes, partners, rank, perm, keys, values):
     near_keys, near_values, *sends = pl.pallas_call(
         functools.partial(first_kernel, sizes, partners),
         out_shape=[pltpu.VMEM(keys.shape, keys.dtype)] * 2
-        + [pltpu.VMEM(sizes.send_shape(), keys.dtype)] * len(partners),
+        + [pltpu.VMEM(sizes.send_shape(m), keys.dtype) for m in partners],
         in_specs=[SMEM, ANY, ANY, ANY],
         out_specs=[VMEM] * (2 + len(partners)),
         scratch_shapes=[
@@ -172,8 +191,8 @@
     copy = pltpu.make_async_copy(queries, near_queries, sem.at[0])
     copy.start()
     rank = rank_ref[0]
-    for d, send in zip(partners, sends):
-        pack_both(sizes, d, rank, perm, keys, values, send)
+    for message, send in zip(partners, sends):
+        pack_both(sizes, message, rank, perm, keys, values, send)
     list_matches(sizes, rank, perm, table, counts)
     squares[...] = jnp.zeros_like(squares)
     copy.wait()
@@ -217,7 +236,7 @@
             pltpu.VMEM((sizes.tokens, sizes.head_dim), jnp.float32),
             jax.ShapeDtypeStruct((sizes.ctx * sizes.capacity,), jnp.int32),
         ]
-        + [pltpu.VMEM(sizes.send_shape(), keys.dtype)] * len(partners),
+        + [pltpu.VMEM(sizes.send_shape(m), keys.dtype) for m in partners],
         in_specs=[SMEM, SMEM, ANY, VMEM, VMEM],
         out_specs=[VMEM] * 5 + [SMEM] + [VMEM] * len(partners),
         scratch_shapes=[
@@ -233,12 +252,12 @@
 
 def update_kernel(sizes, group, partners, last, rank_ref, perm, table, queries, keys, values, *rest):
     before = group == "prev"
-    remote = ["prev"] if before else [d for d in group if d > 0]
+    remote = ["prev"] if before else [m for m in group if m[0] > 0]
     received, rest = dict(zip(remote, rest)), rest[len(remote) + 4 :]
     mixture, weight_sum, peaks, squares = rest[:4]
     rank = rank_ref[0]
-    for d, send in zip(partners, rest[4:]):
-        pack_both(sizes, d, rank, perm, keys, values, send)
+    for message, send in zip(partners, rest[4:]):
+        pack_both(sizes, message, rank, perm, keys, values, send)
 
     def add(here, key_tile, value_tile):
         scores = lax.dot_general(
@@ -270,38 +289,41 @@
 
         return
 
-    def match(d, c, item):
+    def match(message, c, item):
         head = lax.div(item, sizes.blocks * sizes.blocks)
         here = sizes.tile(lax.rem(lax.div(item, sizes.blocks), sizes.blocks), head)
-        if d > 0:
-            add(here, received[d][0, c], received[d][1, c])
+        if message[0] > 0:
+            add(here, *[received[message][i, c - message[1]] for i in range(2)])
         else:
             there = sizes.tile(lax.rem(item, sizes.blocks), head)
             add(here, keys[there], values[there])
 
-    for d in group:
-        for c in range(sizes.capacity):
+    for message in group:
+        d, low, high = message
+        for c in range(low, high):
             item = table[d * sizes.capacity + c]
             if sizes.full:
-                match(d, c, item)
+                match(message, c, item)
             else:
-                pl.when(item >= 0)(functools.partial(match, d, c, item))
+                pl.when(item >= 0)(functools.partial(match, message, c, item))
     if last:
-        rest[4][...] = lax.dot_general(
-            jnp.ones((8, sizes.head_dim), jnp.float32),
-            squares[...],
-            CONTRACT_LAST,
-            precision=lax.Precision.HIGHEST,
-            preferred_element_type=jnp.float32,
-        )[:1]
+        ones = jnp.ones((8, sizes.head_dim), jnp.bfloat16)
+        rest_of = squares[...]
+        total = None
+        for _ in range(3):
+            part = rest_of.astype(jnp.bfloat16)
+            rest_of = rest_of - part.astype(jnp.float32)
+            summed = lax.dot_general(ones, part, CONTRACT_LAST, preferred_element_type=jnp.float32)
+            total = summed if total is None else total + summed
+        rest[4][...] = total[:1]
 
 
 def update(sizes, group, partners, last, rank, perm, table, queries, keys, values, received, state):
-    remote = [received["prev"]] if group == "prev" else [received[d] for d in group if d > 0]
+    remote = ["prev"] if group == "prev" else [m for m in group if m[0] > 0]
+    remote = [received[m] for m in remote]
     arrays = [near(a) for a in [queries, keys, values] + remote + list(state)]
-    count = sizes.heads if group == "prev" else len(group) * sizes.capacity
     out_shape = [pltpu.VMEM(a.shape, a.dtype) for a in state]
-    out_shape += [pltpu.VMEM(sizes.send_shape(), keys.dtype)] * len(partners)
+    out_shape += [pltpu.VMEM(sizes.send_shape(m), keys.dtype) for m in partners]
     if last:
         out_shape.append(jax.ShapeDtypeStruct((1, sizes.tokens), jnp.float32))
     first_state = 3 + len(arrays) - len(state)
@@ -318,17 +340,17 @@
     return tuple(out[:4]), out[4:]
 
 
-def scale_kernel(width, block_len, gain, *rest):
+def scale_kernel(width, step, gain, *rest):
     sums, (attended, out, buffer, sems) = rest[:-4], rest[-4:]
     total = sums[0][...]
     for other in sums[1:]:
         total = total + other[...]
     inverse = lax.rsqrt(total / width + NORM_EPS)
-    steps = attended.shape[0] // block_len
+    steps = attended.shape[0] // step
     copies = []
     for i in range(steps):
-        rows = slice(i * block_len, (i + 1) * block_len)
-        column = jnp.transpose(jnp.broadcast_to(inverse[:, rows], (8, block_len)))[:, :1]
+        rows = slice(i * step, (i + 1) * step)
+        column = jnp.transpose(jnp.broadcast_to(inverse[:, rows], (8, step)))[:, :1]
         buffer[rows] = (attended[rows] * column * gain[...]).astype(out.dtype)
         copies.append(pltpu.make_async_copy(buffer.at[rows], out.at[rows], sems.at[i]))
         copies[i].start()
@@ -336,16 +358,16 @@
         copy.wait()
 
 
-def scaled(attended, sums, gain, width, block_len):
+def scaled(attended, sums, gain, width, step):
     tok_rows, row_width = attended.shape
     return pl.pallas_call(
-        functools.partial(scale_kernel, width, block_len),
+        functools.partial(scale_kernel, width, step),
         out_shape=jax.ShapeDtypeStruct((tok_rows, row_width), jnp.bfloat16),
         in_specs=[VMEM] * (len(sums) + 2),
         out_specs=ANY,
         scratch_shapes=[
             pltpu.VMEM((tok_rows, row_width), jnp.bfloat16),
-            pltpu.SemaphoreType.DMA((tok_rows // block_len,)),
+            pltpu.SemaphoreType.DMA((tok_rows // step,)),
         ],
         compiler_params=PARAMS,
         name="scale_rows",
@@ -359,12 +381,11 @@
     received = {}
 
     def exchange(sends):
-        for d, array in sends.items():
-            with jax.named_scope(f"match{d}"):
-                route = [(i, i ^ d) for i in range(sizes.ctx)]
-                received[d] = lax.ppermute(array, "ctx", route)
-
-    first, steps = schedule(sizes.ctx)
+        for message, array in sends.items():
+            route = [(i, i ^ message[0]) for i in range(sizes.ctx)]
+            received[message] = lax.ppermute(array, "ctx", route)
+
+    first, steps = schedule(sizes.ctx, sizes.capacity)
     last_block = last_blocks(sizes, keys, values)
     keys, values, sends = first_sends(sizes, first, rank, block_perm, keys, values)
     with jax.named_scope("previous"):
@@ -385,7 +406,7 @@
     sums = [extra[-1]]
     for d in range(1, head_size):
         sums.append(lax.ppermute(sums[0], "head", [(i, i ^ d) for i in range(head_size)]))
-    return scaled(state[0], sums, norm_gain, sizes.width * head_size, sizes.block_len)
+    return scaled(state[0], sums, norm_gain, sizes.width * head_size, sizes.block_len // 2)
 
 
 def solution(mesh):

time: 77.3 us -> 76.6 us (level)
  waiting for transfers between devices: 25.1 us -> 14.8 us
  starting transfers between devices: 24.5 us -> 32.3 us
  Pallas kernels: 27.2 us -> 29 us
    ppermute x7 -> x9, waiting for transfers between devices: 21.4 us -> 11.1 us  [exchange(): received[message] = lax.ppermute(array, 'ctx', route)]
    ppermute x7 -> x9, starting transfers between devices: 17.6 us -> 25.4 us  [exchange(): received[message] = lax.ppermute(array, 'ctx', route)]
    pallas_call x7 -> x9, Pallas kernels: 10.7 us -> 12.5 us  [update(): pl.pallas_call(functools.partial(update_kernel, sizes, group, partners, l...]
  transfers between devices with their start and end apart: 11 -> 13, of which waited for: 5 -> 7; matrix products, arithmetic and copies ran while one was open for 0% -> 0% of each run, Pallas kernels for 28% -> 32%
where the time goes in v2:
time: 76.6 us; the launch traced here: 76.4 us
  starting transfers between devices  32.3 us (42%)
  Pallas kernels  29 us (38%)
  waiting for transfers between devices  14.8 us (19%)
    ppermute x9, starting transfers between devices, exchange(): received[message] = lax.ppermute(array, 'ctx', route)  25.4 us
    pallas_call x9, Pallas kernels, update(): pl.pallas_call(functools.partial(update_kernel, sizes, group, partners, l...  12.5 us
    ppermute x9, waiting for transfers between devices, exchange(): received[message] = lax.ppermute(array, 'ctx', route)  11.1 us
    pallas_call x1, Pallas kernels, base(): pl.pallas_call(functools.partial(base_kernel, sizes, partners), out_shape...  10.8 us
    ppermute x3, starting transfers between devices, per_device(): lax.ppermute(sums[0], 'head', [(i, i ^ d) for i in range(head_size)])  4.44 us
    ppermute x3, waiting for transfers between devices, per_device(): lax.ppermute(sums[0], 'head', [(i, i ^ d) for i in range(head_size)])  3.72 us
    pallas_call x1, Pallas kernels, first_sends(): pl.pallas_call(functools.partial(first_kernel, sizes, partners), out_shap...  2.74 us
    ppermute x1, starting transfers between devices, per_device(): received['prev'] = lax.ppermute(last_block, 'ctx', route)  2.42 us
  transfers between devices with their start and end apart: 13, of which 7 were waited for; matrix products, arithmetic and copies ran while one was open for 0% of the time, Pallas kernels for 32%

profile of v2, /device:TPU:0, one launch (start us, length us, event | category | flops | bytes accessed | tf_op | source)
XLA Modules:
  0.0 76.4 jit_solution(10071563403683793201)
XLA Ops:
  0.0 1.2 %last_blocks.1 = bf16[2,256,1024]{2,1,0:T(8,128)(2,1)S(1)} custom-call(bf16[1024,1024]{1,0:T(8,128)(2,1)} %keys.3, bf16[1024,1024]{1,0:T(8,128)(2,1)} %values.3), custom_call_target="tpu_custom_call" | custom-call | flops 1 | bytes 1 | tf_op jit(solution)/shard_map/last_blocks/pallas_call | solution.py:113
  1.2 2.4 %collective-permute-start.2 = (bf16[2,256,1024]{2,1,0:T(8,128)(2,1)S(1)}, bf16[2,256,1024]{2,1,0:T(8,128)(2,1)S(1)}, u32[]{:S(2)}, u32[]{:S(2)}) collective-permute-start(bf16[2,256,1024]{2,1,0:T(8,128)(2,1)S(1)} %last_blocks.1), channel_id=1, source_target_pairs={{0,4},{4,8},{8,12},{12,16},{16,20},{20,24},{24,28},{1,5},{5,9},{9,... | collective-permute-start | bytes 3145736 | tf_op jit(solution)/shard_map/previous/ppermute | solution.py:393
  3.7 2.7 %first_sends.1 = (bf16[1024,1024]{1,0:T(8,128)(2,1)S(1)}, bf16[1024,1024]{1,0:T(8,128)(2,1)S(1)}, bf16[2,4,256,128]{3,2,1,0:T(8,128)(2,1)S(1)}, bf16[2,4,256,128...) custom-call(s32[1]{0:T(128)} %bitcast.1.rank_ref, s32[8,32]{1,0:T(8,128)} %perm.19, ...), custom_call_target="tpu_custom_call" | custom-call | flops 1 | bytes 1 | tf_op jit(solution)/shard_map/first_sends/pallas_call | solution.py:146
  6.4 2.6 %collective-permute-start.1 = (bf16[2,4,256,128]{3,2,1,0:T(8,128)(2,1)S(1)}, bf16[2,4,256,128]{3,2,1,0:T(8,128)(2,1)S(1)}, u32[]{:S(2)}, u32[]{:S(2)}) collective-permute-start(bf16[2,4,256,128]{3,2,1,0:T(8,128)(2,1)S(1)} %get-tuple-element.61), channel_id=1, source_target_pairs={{0,4},{4,0},{8,12},{12,8},{16,20},{20,16},{24,28},{28,24},{1,5},{5... | collective-permute-start | bytes 1572872 | tf_op jit(solution)/shard_map/ppermute | solution.py:386
  9.0 0.9 %collective-permute-start = (bf16[2,4,256,128]{3,2,1,0:T(8,128)(2,1)S(1)}, bf16[2,4,256,128]{3,2,1,0:T(8,128)(2,1)S(1)}, u32[]{:S(2)}, u32[]{:S(2)}) collective-permute-start(bf16[2,4,256,128]{3,2,1,0:T(8,128)(2,1)S(1)} %get-tuple-element.60), channel_id=1, source_target_pairs={{0,24},{4,28},{8,16},{12,20},{16,8},{20,12},{24,0},{28,4},{1,25},{... | collective-permute-start | bytes 1572872 | tf_op jit(solution)/shard_map/ppermute | solution.py:386
  10.0 1.4 %collective-permute-start.4 = (bf16[2,4,256,128]{3,2,1,0:T(8,128)(2,1)S(1)}, bf16[2,4,256,128]{3,2,1,0:T(8,128)(2,1)S(1)}, u32[]{:S(2)}, u32[]{:S(2)}) collective-permute-start(bf16[2,4,256,128]{3,2,1,0:T(8,128)(2,1)S(1)} %get-tuple-element.75), channel_id=1, source_target_pairs={{0,28},{4,24},{8,20},{12,16},{16,12},{20,8},{24,4},{28,0},{1,29},{... | collective-permute-start | bytes 1572872 | tf_op jit(solution)/shard_map/ppermute | solution.py:386
  11.4 1.5 %collective-permute-start.9 = (bf16[2,4,256,128]{3,2,1,0:T(8,128)(2,1)S(1)}, bf16[2,4,256,128]{3,2,1,0:T(8,128)(2,1)S(1)}, u32[]{:S(2)}, u32[]{:S(2)}) collective-permute-start(bf16[2,4,256,128]{3,2,1,0:T(8,128)(2,1)S(1)} %get-tuple-element.84), channel_id=1, source_target_pairs={{0,16},{4,20},{8,24},{12,28},{16,0},{20,4},{24,8},{28,12},{1,17},{... | collective-permute-start | bytes 1572872 | tf_op jit(solution)/shard_map/ppermute | solution.py:386
  12.9 10.8 %base_items.1 = (bf16[1024,1024]{1,0:T(8,128)(2,1)S(1)}, f32[1024,1024]{1,0:T(8,128)S(1)}, f32[1024,1024]{1,0:T(8,128)S(1)}, f32[1024,1024]{1,0:T(8,128)S(1)}, f...) custom-call(s32[1]{0:T(128)} %bitcast.1.rank_ref, s32[8,32]{1,0:T(8,128)S(1)} %copy-done, ...), custom_call_target="tpu_custom_call" | custom-call | flops 1 | bytes 1 | tf_op jit(solution)/shard_map/base_items/pallas_call | solution.py:229
  23.7 3.3 %collective-permute-start.8 = (bf16[2,4,256,128]{3,2,1,0:T(8,128)(2,1)S(1)}, bf16[2,4,256,128]{3,2,1,0:T(8,128)(2,1)S(1)}, u32[]{:S(2)}, u32[]{:S(2)}) collective-permute-start(bf16[2,4,256,128]{3,2,1,0:T(8,128)(2,1)S(1)} %get-tuple-element.83), channel_id=1, source_target_pairs={{0,8},{4,12},{8,0},{12,4},{16,24},{20,28},{24,16},{28,20},{1,9},{5... | collective-permute-start | bytes 1572872 | tf_op jit(solution)/shard_map/ppermute | solution.py:386
  27.0 0.8 %update_items.9 = (f32[1024,1024]{1,0:T(8,128)S(1)}, f32[1024,1024]{1,0:T(8,128)S(1)}, f32[1024,1024]{1,0:T(8,128)S(1)}, f32[1024,128]{1,0:T(8,128)S(1)}, bf16[2,2,256,128]{3,2,1,0:T(8,128)(2,1)S(1)}) custom-call(s32[1]{0:T(128)} %bitcast.1.rank_ref, s32[8,32]{1,0:T(8,128)S(1)} %copy-done, ...), custom_call_target="tpu_custom_call", output_to_operand_aliasing={{0}: (7, {}), {1}: (8, {}), {2}: (9, {}), {3}: (10, {})} | custom-call | flops 1 | bytes 1 | tf_op jit(solution)/shard_map/update_items/pallas_call | solution.py:330
  27.9 0.1 collective-permute-start.7
  27.9 2.1 %update_items.10 = (f32[1024,1024]{1,0:T(8,128)S(1)}, f32[1024,1024]{1,0:T(8,128)S(1)}, f32[1024,1024]{1,0:T(8,128)S(1)}, f32[1024,128]{1,0:T(8,128)S(1)}, bf16[2,2,256,128]{3,2,1,0:T(8,128)(2,1)S(1)}) custom-call(s32[1]{0:T(128)} %bitcast.1.rank_ref, s32[8,32]{1,0:T(8,128)S(1)} %copy-done, ...), custom_call_target="tpu_custom_call", output_to_operand_aliasing={{0}: (7, {}), {1}: (8, {}), {2}: (9, {}), {3}: (10, {})} | custom-call | flops 1 | bytes 1 | tf_op jit(solution)/shard_map/update_items/pallas_call | solution.py:330
  30.0 0.0 collective-permute-done.rest_0_
  30.0 1.5 %update_items.11 = (f32[1024,1024]{1,0:T(8,128)S(1)}, f32[1024,1024]{1,0:T(8,128)S(1)}, f32[1024,1024]{1,0:T(8,128)S(1)}, f32[1024,128]{1,0:T(8,128)S(1)}, bf16[2,2,256,128]{3,2,1,0:T(8,128)(2,1)S(1)}) custom-call(s32[1]{0:T(128)} %bitcast.1.rank_ref, s32[8,32]{1,0:T(8,128)S(1)} %copy-done, ...), custom_call_target="tpu_custom_call", output_to_operand_aliasing={{0}: (7, {}), {1}: (8, {}), {2}: (9, {}), {3}: (10, {})} | custom-call | flops 1 | bytes 1 | tf_op jit(solution)/shard_map/update_items/pallas_call | solution.py:330
  31.5 8.1 %collective-permute-start.3 = (bf16[2,2,256,128]{3,2,1,0:T(8,128)(2,1)S(1)}, bf16[2,2,256,128]{3,2,1,0:T(8,128)(2,1)S(1)}, u32[]{:S(2)}, u32[]{:S(2)}) collective-permute-start(bf16[2,2,256,128]{3,2,1,0:T(8,128)(2,1)S(1)} %get-tuple-element.74), channel_id=1, source_target_pairs={{0,20},{4,16},{8,28},{12,24},{16,4},{20,0},{24,12},{28,8},{1,21},{... | collective-permute-start | bytes 786440 | tf_op jit(solution)/shard_map/ppermute | solution.py:386
  39.6 7.5 %collective-permute-start.6 = (bf16[2,2,256,128]{3,2,1,0:T(8,128)(2,1)S(1)}, bf16[2,2,256,128]{3,2,1,0:T(8,128)(2,1)S(1)}, u32[]{:S(2)}, u32[]{:S(2)}) collective-permute-start(bf16[2,2,256,128]{3,2,1,0:T(8,128)(2,1)S(1)} %get-tuple-element.81), channel_id=1, source_target_pairs={{0,12},{4,8},{8,4},{12,0},{16,28},{20,24},{24,20},{28,16},{1,13},{... | collective-permute-start | bytes 786440 | tf_op jit(solution)/shard_map/ppermute | solution.py:386
  47.2 1.7 %update_items.12 = (f32[1024,1024]{1,0:T(8,128)S(1)}, f32[1024,1024]{1,0:T(8,128)S(1)}, f32[1024,1024]{1,0:T(8,128)S(1)}, f32[1024,128]{1,0:T(8,128)S(1)}, bf16[2,2,256,128]{3,2,1,0:T(8,128)(2,1)S(1)}) custom-call(s32[1]{0:T(128)} %bitcast.1.rank_ref, s32[8,32]{1,0:T(8,128)S(1)} %copy-done, ...), custom_call_target="tpu_custom_call", output_to_operand_aliasing={{0}: (7, {}), {1}: (8, {}), {2}: (9, {}), {3}: (10, {})} | custom-call | flops 1 | bytes 1 | tf_op jit(solution)/shard_map/update_items/pallas_call | solution.py:330
  48.9 3.6 %collective-permute-done.9.rest_0_ = bf16[2,4,256,128]{3,2,1,0:T(8,128)(2,1)S(1)} collective-permute-done((bf16[2,4,256,128]{3,2,1,0:T(8,128)(2,1)S(1)}, bf16[2,4,256,128]{3,2,1,0:T(8,128)(2,1)S(1)}, u32[]{:S(2)}, u32[]{:S(2)}) %collective-permute-start.9) | collective-permute-done | bytes 524320 | tf_op jit(solution)/shard_map/ppermute | solution.py:386
  52.5 1.3 %update_items.13 = (f32[1024,1024]{1,0:T(8,128)S(1)}, f32[1024,1024]{1,0:T(8,128)S(1)}, f32[1024,1024]{1,0:T(8,128)S(1)}, f32[1024,128]{1,0:T(8,128)S(1)}) custom-call(s32[1]{0:T(128)} %bitcast.1.rank_ref, s32[8,32]{1,0:T(8,128)S(1)} %copy-done, ...), custom_call_target="tpu_custom_call", output_to_operand_aliasing={{0}: (7, {}), {1}: (8, {}), {2}: (9, {}), {3}: (10, {})} | custom-call | flops 1 | bytes 1 | tf_op jit(solution)/shard_map/update_items/pallas_call | solution.py:330
  53.8 1.3 %update_items.14 = (f32[1024,1024]{1,0:T(8,128)S(1)}, f32[1024,1024]{1,0:T(8,128)S(1)}, f32[1024,1024]{1,0:T(8,128)S(1)}, f32[1024,128]{1,0:T(8,128)S(1)}) custom-call(s32[1]{0:T(128)} %bitcast.1.rank_ref, s32[8,32]{1,0:T(8,128)S(1)} %copy-done, ...), custom_call_target="tpu_custom_call", output_to_operand_aliasing={{0}: (7, {}), {1}: (8, {}), {2}: (9, {}), {3}: (10, {})} | custom-call | flops 1 | bytes 1 | tf_op jit(solution)/shard_map/update_items/pallas_call | solution.py:330
  55.1 3.0 %collective-permute-done.7.rest_0_ = bf16[2,2,256,128]{3,2,1,0:T(8,128)(2,1)S(1)} collective-permute-done((bf16[2,2,256,128]{3,2,1,0:T(8,128)(2,1)S(1)}, bf16[2,2,256,128]{3,2,1,0:T(8,128)(2,1)S(1)}, u32[]{:S(2)}, u32[]{:S(2)}) %collective-permute-start.7) | collective-permute-done | bytes 262176 | tf_op jit(solution)/shard_map/ppermute | solution.py:386
  58.1 1.1 %update_items.15 = (f32[1024,1024]{1,0:T(8,128)S(1)}, f32[1024,1024]{1,0:T(8,128)S(1)}, f32[1024,1024]{1,0:T(8,128)S(1)}, f32[1024,128]{1,0:T(8,128)S(1)}) custom-call(s32[1]{0:T(128)} %bitcast.1.rank_ref, s32[8,32]{1,0:T(8,128)S(1)} %copy-done, ...), custom_call_target="tpu_custom_call", output_to_operand_aliasing={{0}: (7, {}), {1}: (8, {}), {2}: (9, {}), {3}: (10, {})} | custom-call | flops 1 | bytes 1 | tf_op jit(solution)/shard_map/update_items/pallas_call | solution.py:330
  59.2 2.4 %collective-permute-done.6.rest_0_ = bf16[2,2,256,128]{3,2,1,0:T(8,128)(2,1)S(1)} collective-permute-done((bf16[2,2,256,128]{3,2,1,0:T(8,128)(2,1)S(1)}, bf16[2,2,256,128]{3,2,1,0:T(8,128)(2,1)S(1)}, u32[]{:S(2)}, u32[]{:S(2)}) %collective-permute-start.6) | collective-permute-done | bytes 262176 | tf_op jit(solution)/shard_map/ppermute | solution.py:386
  61.6 1.1 %update_items.16 = (f32[1024,1024]{1,0:T(8,128)S(1)}, f32[1024,1024]{1,0:T(8,128)S(1)}, f32[1024,1024]{1,0:T(8,128)S(1)}, f32[1024,128]{1,0:T(8,128)S(1)}) custom-call(s32[1]{0:T(128)} %bitcast.1.rank_ref, s32[8,32]{1,0:T(8,128)S(1)} %copy-done, ...), custom_call_target="tpu_custom_call", output_to_operand_aliasing={{0}: (7, {}), {1}: (8, {}), {2}: (9, {}), {3}: (10, {})} | custom-call | flops 1 | bytes 1 | tf_op jit(solution)/shard_map/update_items/pallas_call | solution.py:330
  62.7 1.0 %collective-permute-done.3.rest_0_ = bf16[2,2,256,128]{3,2,1,0:T(8,128)(2,1)S(1)} collective-permute-done((bf16[2,2,256,128]{3,2,1,0:T(8,128)(2,1)S(1)}, bf16[2,2,256,128]{3,2,1,0:T(8,128)(2,1)S(1)}, u32[]{:S(2)}, u32[]{:S(2)}) %collective-permute-start.3) | collective-permute-done | bytes 262176 | tf_op jit(solution)/shard_map/ppermute | solution.py:386
  63.7 1.0 %collective-permute-done.5.rest_1_ = bf16[2,2,256,128]{3,2,1,0:T(8,128)(2,1)S(1)} collective-permute-done((bf16[2,2,256,128]{3,2,1,0:T(8,128)(2,1)S(1)}, bf16[2,2,256,128]{3,2,1,0:T(8,128)(2,1)S(1)}, u32[]{:S(2)}, u32[]{:S(2)}) %collective-permute-start.5) | collective-permute-done | bytes 262176 | tf_op jit(solution)/shard_map/ppermute | solution.py:386
  64.7 1.6 %update_items.17 = (f32[1024,1024]{1,0:T(8,128)S(1)}, f32[1024,1024]{1,0:T(8,128)S(1)}, f32[1024,1024]{1,0:T(8,128)S(1)}, f32[1024,128]{1,0:T(8,128)S(1)}, f32[1,1024]{1,0:T(1,128)S(1)}) custom-call(s32[1]{0:T(128)} %bitcast.1.rank_ref, s32[8,32]{1,0:T(8,128)S(1)} %copy-done, ...), custom_call_target="tpu_custom_call", output_to_operand_aliasing={{0}: (8, {}), {1}: (9, {}), {2}: (10, {}), {3}: (11, {})} | custom-call | flops 1 | bytes 1 | tf_op jit(solution)/shard_map/update_items/pallas_call | solution.py:330
  66.4 3.7 %collective-permute-start.12 = (f32[1,1024]{1,0:T(1,128)S(1)}, f32[1,1024]{1,0:T(1,128)S(1)}, u32[]{:S(2)}, u32[]{:S(2)}) collective-permute-start(f32[1,1024]{1,0:T(1,128)S(1)} %get-tuple-element.105.rest_0_), channel_id=1, source_target_pairs={{0,3},{1,2},{2,1},{3,0},{4,7},{5,6},{6,5},{7,4},{8,11},{9,10},{10,... | collective-permute-start | bytes 12296 | tf_op jit(solution)/shard_map/ppermute | solution.py:408
  70.0 0.8 %collective-permute-start.10 = (f32[1,1024]{1,0:T(1,128)S(1)}, f32[1,1024]{1,0:T(1,128)S(1)}, u32[]{:S(2)}, u32[]{:S(2)}) collective-permute-start(f32[1,1024]{1,0:T(1,128)S(1)} %get-tuple-element.105.rest_0_), channel_id=1, source_target_pairs={{0,1},{1,0},{2,3},{3,2},{4,5},{5,4},{6,7},{7,6},{8,9},{9,8},{10,11... | collective-permute-start | bytes 12296 | tf_op jit(solution)/shard_map/ppermute | solution.py:408
  70.8 1.0 %collective-permute-done.12.rest_3_ = f32[1,1024]{1,0:T(1,128)S(1)} collective-permute-done((f32[1,1024]{1,0:T(1,128)S(1)}, f32[1,1024]{1,0:T(1,128)S(1)}, u32[]{:S(2)}, u32[]{:S(2)}) %collective-permute-start.12) | collective-permute-done | bytes 4128 | tf_op jit(solution)/shard_map/ppermute | solution.py:408
  71.8 2.7 %collective-permute-done.11.rest_2_ = f32[1,1024]{1,0:T(1,128)S(1)} collective-permute-done((f32[1,1024]{1,0:T(1,128)S(1)}, f32[1,1024]{1,0:T(1,128)S(1)}, u32[]{:S(2)}, u32[]{:S(2)}) %collective-permute-start.11) | collective-permute-done | bytes 4128 | tf_op jit(solution)/shard_map/ppermute | solution.py:408
  74.5 1.7 %scale_rows.1 = bf16[1024,1024]{1,0:T(8,128)(2,1)} custom-call(f32[1,1024]{1,0:T(1,128)S(1)} %bitcast.2, f32[1,1024]{1,0:T(1,128)S(1)} %get-tuple-element.105.rest_0_, f32[1,1024]{1,0:T(1,128)S(1)} %collective-permute-done.10.rest_1_, f32[1,1024]{1,0:T(1,128)S(1)} %collective-permute-done.11.rest_2_, f32[1,1024]{1,0:T(1,128)S(1)} %collective-permute-done.12.rest_3_, ...), custom_call_target="tpu_custom_call" | custom-call | tf_op jit(solution)/shard_map/scale_rows/pallas_call | solution.py:363
  (11 shorter events, 0.0 us)
Async XLA Ops:
  0.0 12.9 %copy-start = (s32[8,32]{1,0:T(8,128)S(1)}, s32[8,32]{1,0:T(8,128)}, u32[]{:S(2)}) copy-start(s32[8,32]{1,0:T(8,128)} %perm.19) | copy-start | bytes 3076
  1.2 22.5 %collective-permute-start.2 = (bf16[2,256,1024]{2,1,0:T(8,128)(2,1)S(1)}, bf16[2,256,1024]{2,1,0:T(8,128)(2,1)S(1)}, u32[]{:S(2)}, u32[]{:S(2)}) collective-permute-start(bf16[2,256,1024]{2,1,0:T(8,128)(2,1)S(1)} %last_blocks.1), channel_id=1, source_target_pairs={{0,4},{4,8},{8,12},{12,16},{16,20},{20,24},{24,28},{1,5},{5,9},{9,... | collective-permute-start | bytes 3145736 | tf_op jit(solution)/shard_map/previous/ppermute | solution.py:393
  6.4 21.4 %collective-permute-start.1 = (bf16[2,4,256,128]{3,2,1,0:T(8,128)(2,1)S(1)}, bf16[2,4,256,128]{3,2,1,0:T(8,128)(2,1)S(1)}, u32[]{:S(2)}, u32[]{:S(2)}) collective-permute-start(bf16[2,4,256,128]{3,2,1,0:T(8,128)(2,1)S(1)} %get-tuple-element.61), channel_id=1, source_target_pairs={{0,4},{4,0},{8,12},{12,8},{16,20},{20,16},{24,28},{28,24},{1,5},{5... | collective-permute-start | bytes 1572872 | tf_op jit(solution)/shard_map/ppermute | solution.py:386
  9.0 21.0 %collective-permute-start = (bf16[2,4,256,128]{3,2,1,0:T(8,128)(2,1)S(1)}, bf16[2,4,256,128]{3,2,1,0:T(8,128)(2,1)S(1)}, u32[]{:S(2)}, u32[]{:S(2)}) collective-permute-start(bf16[2,4,256,128]{3,2,1,0:T(8,128)(2,1)S(1)} %get-tuple-element.60), channel_id=1, source_target_pairs={{0,24},{4,28},{8,16},{12,20},{16,8},{20,12},{24,0},{28,4},{1,25},{... | collective-permute-start | bytes 1572872 | tf_op jit(solution)/shard_map/ppermute | solution.py:386
  10.0 29.7 %collective-permute-start.4 = (bf16[2,4,256,128]{3,2,1,0:T(8,128)(2,1)S(1)}, bf16[2,4,256,128]{3,2,1,0:T(8,128)(2,1)S(1)}, u32[]{:S(2)}, u32[]{:S(2)}) collective-permute-start(bf16[2,4,256,128]{3,2,1,0:T(8,128)(2,1)S(1)} %get-tuple-element.75), channel_id=1, source_target_pairs={{0,28},{4,24},{8,20},{12,16},{16,12},{20,8},{24,4},{28,0},{1,29},{... | collective-permute-start | bytes 1572872 | tf_op jit(solution)/shard_map/ppermute | solution.py:386
  11.4 41.1 %collective-permute-start.9 = (bf16[2,4,256,128]{3,2,1,0:T(8,128)(2,1)S(1)}, bf16[2,4,256,128]{3,2,1,0:T(8,128)(2,1)S(1)}, u32[]{:S(2)}, u32[]{:S(2)}) collective-permute-start(bf16[2,4,256,128]{3,2,1,0:T(8,128)(2,1)S(1)} %get-tuple-element.84), channel_id=1, source_target_pairs={{0,16},{4,20},{8,24},{12,28},{16,0},{20,4},{24,8},{28,12},{1,17},{... | collective-permute-start | bytes 1572872 | tf_op jit(solution)/shard_map/ppermute | solution.py:386
  23.7 30.1 %collective-permute-start.8 = (bf16[2,4,256,128]{3,2,1,0:T(8,128)(2,1)S(1)}, bf16[2,4,256,128]{3,2,1,0:T(8,128)(2,1)S(1)}, u32[]{:S(2)}, u32[]{:S(2)}) collective-permute-start(bf16[2,4,256,128]{3,2,1,0:T(8,128)(2,1)S(1)} %get-tuple-element.83), channel_id=1, source_target_pairs={{0,8},{4,12},{8,0},{12,4},{16,24},{20,28},{24,16},{28,20},{1,9},{5... | collective-permute-start | bytes 1572872 | tf_op jit(solution)/shard_map/ppermute | solution.py:386
  27.9 30.2 %collective-permute-start.7 = (bf16[2,2,256,128]{3,2,1,0:T(8,128)(2,1)S(1)}, bf16[2,2,256,128]{3,2,1,0:T(8,128)(2,1)S(1)}, u32[]{:S(2)}, u32[]{:S(2)}) collective-permute-start(bf16[2,2,256,128]{3,2,1,0:T(8,128)(2,1)S(1)} %get-tuple-element.82), channel_id=1, source_target_pairs={{0,20},{4,16},{8,28},{12,24},{16,4},{20,0},{24,12},{28,8},{1,21},{... | collective-permute-start | bytes 786440 | tf_op jit(solution)/shard_map/ppermute | solution.py:386
  31.5 32.2 %collective-permute-start.3 = (bf16[2,2,256,128]{3,2,1,0:T(8,128)(2,1)S(1)}, bf16[2,2,256,128]{3,2,1,0:T(8,128)(2,1)S(1)}, u32[]{:S(2)}, u32[]{:S(2)}) collective-permute-start(bf16[2,2,256,128]{3,2,1,0:T(8,128)(2,1)S(1)} %get-tuple-element.74), channel_id=1, source_target_pairs={{0,20},{4,16},{8,28},{12,24},{16,4},{20,0},{24,12},{28,8},{1,21},{... | collective-permute-start | bytes 786440 | tf_op jit(solution)/shard_map/ppermute | solution.py:386
  39.6 21.9 %collective-permute-start.6 = (bf16[2,2,256,128]{3,2,1,0:T(8,128)(2,1)S(1)}, bf16[2,2,256,128]{3,2,1,0:T(8,128)(2,1)S(1)}, u32[]{:S(2)}, u32[]{:S(2)}) collective-permute-start(bf16[2,2,256,128]{3,2,1,0:T(8,128)(2,1)S(1)} %get-tuple-element.81), channel_id=1, source_target_pairs={{0,12},{4,8},{8,4},{12,0},{16,28},{20,24},{24,20},{28,16},{1,13},{... | collective-permute-start | bytes 786440 | tf_op jit(solution)/shard_map/ppermute | solution.py:386
  52.5 12.3 %collective-permute-start.5 = (bf16[2,2,256,128]{3,2,1,0:T(8,128)(2,1)S(1)}, bf16[2,2,256,128]{3,2,1,0:T(8,128)(2,1)S(1)}, u32[]{:S(2)}, u32[]{:S(2)}) collective-permute-start(bf16[2,2,256,128]{3,2,1,0:T(8,128)(2,1)S(1)} %get-tuple-element.80), channel_id=1, source_target_pairs={{0,12},{4,8},{8,4},{12,0},{16,28},{20,24},{24,20},{28,16},{1,13},{... | collective-permute-start | bytes 786440 | tf_op jit(solution)/shard_map/ppermute | solution.py:386
  64.7 9.8 %copy-start.1 = (f32[1024]{0:T(1024)S(1)}, f32[1024]{0:T(1024)}, u32[]{:S(2)}) copy-start(f32[1024]{0:T(1024)} %param.9) | copy-start | bytes 12292
  66.4 5.5 %collective-permute-start.12 = (f32[1,1024]{1,0:T(1,128)S(1)}, f32[1,1024]{1,0:T(1,128)S(1)}, u32[]{:S(2)}, u32[]{:S(2)}) collective-permute-start(f32[1,1024]{1,0:T(1,128)S(1)} %get-tuple-element.105.rest_0_), channel_id=1, source_target_pairs={{0,3},{1,2},{2,1},{3,0},{4,7},{5,6},{6,5},{7,4},{8,11},{9,10},{10,... | collective-permute-start | bytes 12296 | tf_op jit(solution)/shard_map/ppermute | solution.py:408
  70.0 4.5 %collective-permute-start.11 = (f32[1,1024]{1,0:T(1,128)S(1)}, f32[1,1024]{1,0:T(1,128)S(1)}, u32[]{:S(2)}, u32[]{:S(2)}) collective-permute-start(f32[1,1024]{1,0:T(1,128)S(1)} %get-tuple-element.105.rest_0_), channel_id=1, source_target_pairs={{0,2},{1,3},{2,0},{3,1},{4,6},{5,7},{6,4},{7,5},{8,10},{9,11},{10,... | collective-permute-start | bytes 12296 | tf_op jit(solution)/shard_map/ppermute | solution.py:408
  70.0 4.5 %collective-permute-start.10 = (f32[1,1024]{1,0:T(1,128)S(1)}, f32[1,1024]{1,0:T(1,128)S(1)}, u32[]{:S(2)}, u32[]{:S(2)}) collective-permute-start(f32[1,1024]{1,0:T(1,128)S(1)} %get-tuple-element.105.rest_0_), channel_id=1, source_target_pairs={{0,1},{1,0},{2,3},{3,2},{4,5},{5,4},{6,7},{7,6},{8,9},{9,8},{10,11... | collective-permute-start | bytes 12296 | tf_op jit(solution)/shard_map/ppermute | solution.py:408

commit v3 on v2

--- a/solution.py
+++ b/solution.py
@@ -54,7 +54,8 @@
             ((whole[2],), []),
             ((five,), []),
             ((three,), []),
-            ((last_five, last_three), []),
+            ((last_five,), []),
+            ((last_three,), []),
         ]
         return [whole[d] for d in (6, 7, 4, 1)], steps
     rest = [whole[d] for d in range(1, ctx)]
@@ -404,7 +405,7 @@
         )
         exchange(dict(zip(partners, extra)))
     sums = [extra[-1]]
-    for d in range(1, head_size):
+    for d in sorted(range(1, head_size), key=lambda d: (d % 2 == 0, d)):
         sums.append(lax.ppermute(sums[0], "head", [(i, i ^ d) for i in range(head_size)]))
     return scaled(state[0], sums, norm_gain, sizes.width * head_size, sizes.block_len // 2)
 

time: 76.6 us -> 76.4 us (level)
  waiting for transfers between devices: 14.8 us -> 13.2 us
  Pallas kernels: 29 us -> 29.9 us
    ppermute x9, waiting for transfers between devices: 11.1 us -> 9.41 us  [exchange(): received[message] = lax.ppermute(array, 'ctx', route)]
    pallas_call x9 -> x10, Pallas kernels: 12.5 us -> 13.4 us  [update(): pl.pallas_call(functools.partial(update_kernel, sizes, group, partners, l...]
  transfers between devices with their start and end apart: 13 -> 13, of which waited for: 7 -> 6; matrix products, arithmetic and copies ran while one was open for 0% -> 0% of each run, Pallas kernels for 32% -> 34%
where the time goes in v3:
time: 76.4 us; the launch traced here: 76.2 us
  starting transfers between devices  32.7 us (43%)
  Pallas kernels  29.9 us (39%)
  waiting for transfers between devices  13.2 us (17%)
    ppermute x9, starting transfers between devices, exchange(): received[message] = lax.ppermute(array, 'ctx', route)  26.1 us
    pallas_call x10, Pallas kernels, update(): pl.pallas_call(functools.partial(update_kernel, sizes, group, partners, l...  13.4 us
    pallas_call x1, Pallas kernels, base(): pl.pallas_call(functools.partial(base_kernel, sizes, partners), out_shape...  10.8 us
    ppermute x9, waiting for transfers between devices, exchange(): received[message] = lax.ppermute(array, 'ctx', route)  9.41 us
    ppermute x3, starting transfers between devices, per_device(): lax.ppermute(sums[0], 'head', [(i, i ^ d) for i in range(head_size)])  4.22 us
    ppermute x3, waiting for transfers between devices, per_device(): lax.ppermute(sums[0], 'head', [(i, i ^ d) for i in range(head_size)])  3.83 us
    pallas_call x1, Pallas kernels, first_sends(): pl.pallas_call(functools.partial(first_kernel, sizes, partners), out_shap...  2.74 us
    ppermute x1, starting transfers between devices, per_device(): received['prev'] = lax.ppermute(last_block, 'ctx', route)  2.42 us
  transfers between devices with their start and end apart: 13, of which 6 were waited for; matrix products, arithmetic and copies ran while one was open for 0% of the time, Pallas kernels for 34%

profile of v3, /device:TPU:0, one launch (start us, length us, event | category | flops | bytes accessed | tf_op | source)
XLA Modules:
  0.0 76.2 jit_solution(11552953049951893755)
XLA Ops:
  0.0 1.2 %last_blocks.1 = bf16[2,256,1024]{2,1,0:T(8,128)(2,1)S(1)} custom-call(bf16[1024,1024]{1,0:T(8,128)(2,1)} %keys.3, bf16[1024,1024]{1,0:T(8,128)(2,1)} %values.3), custom_call_target="tpu_custom_call" | custom-call | flops 1 | bytes 1 | tf_op jit(solution)/shard_map/last_blocks/pallas_call | solution.py:114
  1.2 2.4 %collective-permute-start.3 = (bf16[2,256,1024]{2,1,0:T(8,128)(2,1)S(1)}, bf16[2,256,1024]{2,1,0:T(8,128)(2,1)S(1)}, u32[]{:S(2)}, u32[]{:S(2)}) collective-permute-start(bf16[2,256,1024]{2,1,0:T(8,128)(2,1)S(1)} %last_blocks.1), channel_id=1, source_target_pairs={{0,4},{4,8},{8,12},{12,16},{16,20},{20,24},{24,28},{1,5},{5,9},{9,... | collective-permute-start | bytes 3145736 | tf_op jit(solution)/shard_map/previous/ppermute | solution.py:394
  3.7 2.7 %first_sends.1 = (bf16[1024,1024]{1,0:T(8,128)(2,1)S(1)}, bf16[1024,1024]{1,0:T(8,128)(2,1)S(1)}, bf16[2,4,256,128]{3,2,1,0:T(8,128)(2,1)S(1)}, bf16[2,4,256,128...) custom-call(s32[1]{0:T(128)} %bitcast.1.rank_ref, s32[8,32]{1,0:T(8,128)} %perm.21, ...), custom_call_target="tpu_custom_call" | custom-call | flops 1 | bytes 1 | tf_op jit(solution)/shard_map/first_sends/pallas_call | solution.py:147
  6.4 2.6 %collective-permute-start.2 = (bf16[2,4,256,128]{3,2,1,0:T(8,128)(2,1)S(1)}, bf16[2,4,256,128]{3,2,1,0:T(8,128)(2,1)S(1)}, u32[]{:S(2)}, u32[]{:S(2)}) collective-permute-start(bf16[2,4,256,128]{3,2,1,0:T(8,128)(2,1)S(1)} %get-tuple-element.66), channel_id=1, source_target_pairs={{0,4},{4,0},{8,12},{12,8},{16,20},{20,16},{24,28},{28,24},{1,5},{5... | collective-permute-start | bytes 1572872 | tf_op jit(solution)/shard_map/ppermute | solution.py:387
  9.0 0.9 %collective-permute-start.1 = (bf16[2,4,256,128]{3,2,1,0:T(8,128)(2,1)S(1)}, bf16[2,4,256,128]{3,2,1,0:T(8,128)(2,1)S(1)}, u32[]{:S(2)}, u32[]{:S(2)}) collective-permute-start(bf16[2,4,256,128]{3,2,1,0:T(8,128)(2,1)S(1)} %get-tuple-element.65), channel_id=1, source_target_pairs={{0,24},{4,28},{8,16},{12,20},{16,8},{20,12},{24,0},{28,4},{1,25},{... | collective-permute-start | bytes 1572872 | tf_op jit(solution)/shard_map/ppermute | solution.py:387
  10.0 1.4 %collective-permute-start = (bf16[2,4,256,128]{3,2,1,0:T(8,128)(2,1)S(1)}, bf16[2,4,256,128]{3,2,1,0:T(8,128)(2,1)S(1)}, u32[]{:S(2)}, u32[]{:S(2)}) collective-permute-start(bf16[2,4,256,128]{3,2,1,0:T(8,128)(2,1)S(1)} %get-tuple-element.64), channel_id=1, source_target_pairs={{0,28},{4,24},{8,20},{12,16},{16,12},{20,8},{24,4},{28,0},{1,29},{... | collective-permute-start | bytes 1572872 | tf_op jit(solution)/shard_map/ppermute | solution.py:387
  11.4 1.5 %collective-permute-start.9 = (bf16[2,4,256,128]{3,2,1,0:T(8,128)(2,1)S(1)}, bf16[2,4,256,128]{3,2,1,0:T(8,128)(2,1)S(1)}, u32[]{:S(2)}, u32[]{:S(2)}) collective-permute-start(bf16[2,4,256,128]{3,2,1,0:T(8,128)(2,1)S(1)} %get-tuple-element.88), channel_id=1, source_target_pairs={{0,16},{4,20},{8,24},{12,28},{16,0},{20,4},{24,8},{28,12},{1,17},{... | collective-permute-start | bytes 1572872 | tf_op jit(solution)/shard_map/ppermute | solution.py:387
  12.9 10.8 %base_items.1 = (bf16[1024,1024]{1,0:T(8,128)(2,1)S(1)}, f32[1024,1024]{1,0:T(8,128)S(1)}, f32[1024,1024]{1,0:T(8,128)S(1)}, f32[1024,1024]{1,0:T(8,128)S(1)}, f...) custom-call(s32[1]{0:T(128)} %bitcast.1.rank_ref, s32[8,32]{1,0:T(8,128)S(1)} %copy-done, ...), custom_call_target="tpu_custom_call" | custom-call | flops 1 | bytes 1 | tf_op jit(solution)/shard_map/base_items/pallas_call | solution.py:230
  23.7 3.3 %collective-permute-start.8 = (bf16[2,4,256,128]{3,2,1,0:T(8,128)(2,1)S(1)}, bf16[2,4,256,128]{3,2,1,0:T(8,128)(2,1)S(1)}, u32[]{:S(2)}, u32[]{:S(2)}) collective-permute-start(bf16[2,4,256,128]{3,2,1,0:T(8,128)(2,1)S(1)} %get-tuple-element.87), channel_id=1, source_target_pairs={{0,8},{4,12},{8,0},{12,4},{16,24},{20,28},{24,16},{28,20},{1,9},{5... | collective-permute-start | bytes 1572872 | tf_op jit(solution)/shard_map/ppermute | solution.py:387
  27.0 0.8 %update_items.10 = (f32[1024,1024]{1,0:T(8,128)S(1)}, f32[1024,1024]{1,0:T(8,128)S(1)}, f32[1024,1024]{1,0:T(8,128)S(1)}, f32[1024,128]{1,0:T(8,128)S(1)}, bf16[2,2,256,128]{3,2,1,0:T(8,128)(2,1)S(1)}) custom-call(s32[1]{0:T(128)} %bitcast.1.rank_ref, s32[8,32]{1,0:T(8,128)S(1)} %copy-done, ...), custom_call_target="tpu_custom_call", output_to_operand_aliasing={{0}: (7, {}), {1}: (8, {}), {2}: (9, {}), {3}: (10, {})} | custom-call | flops 1 | bytes 1 | tf_op jit(solution)/shard_map/update_items/pallas_call | solution.py:331
  27.9 0.1 collective-permute-start.7
  27.9 2.1 %update_items.11 = (f32[1024,1024]{1,0:T(8,128)S(1)}, f32[1024,1024]{1,0:T(8,128)S(1)}, f32[1024,1024]{1,0:T(8,128)S(1)}, f32[1024,128]{1,0:T(8,128)S(1)}, bf16[2,2,256,128]{3,2,1,0:T(8,128)(2,1)S(1)}) custom-call(s32[1]{0:T(128)} %bitcast.1.rank_ref, s32[8,32]{1,0:T(8,128)S(1)} %copy-done, ...), custom_call_target="tpu_custom_call", output_to_operand_aliasing={{0}: (7, {}), {1}: (8, {}), {2}: (9, {}), {3}: (10, {})} | custom-call | flops 1 | bytes 1 | tf_op jit(solution)/shard_map/update_items/pallas_call | solution.py:331
  30.0 8.1 %collective-permute-start.6 = (bf16[2,2,256,128]{3,2,1,0:T(8,128)(2,1)S(1)}, bf16[2,2,256,128]{3,2,1,0:T(8,128)(2,1)S(1)}, u32[]{:S(2)}, u32[]{:S(2)}) collective-permute-start(bf16[2,2,256,128]{3,2,1,0:T(8,128)(2,1)S(1)} %get-tuple-element.85), channel_id=1, source_target_pairs={{0,12},{4,8},{8,4},{12,0},{16,28},{20,24},{24,20},{28,16},{1,13},{... | collective-permute-start | bytes 786440 | tf_op jit(solution)/shard_map/ppermute | solution.py:387
  38.2 1.5 %update_items.12 = (f32[1024,1024]{1,0:T(8,128)S(1)}, f32[1024,1024]{1,0:T(8,128)S(1)}, f32[1024,1024]{1,0:T(8,128)S(1)}, f32[1024,128]{1,0:T(8,128)S(1)}, bf16[2,2,256,128]{3,2,1,0:T(8,128)(2,1)S(1)}) custom-call(s32[1]{0:T(128)} %bitcast.1.rank_ref, s32[8,32]{1,0:T(8,128)S(1)} %copy-done, ...), custom_call_target="tpu_custom_call", output_to_operand_aliasing={{0}: (7, {}), {1}: (8, {}), {2}: (9, {}), {3}: (10, {})} | custom-call | flops 1 | bytes 1 | tf_op jit(solution)/shard_map/update_items/pallas_call | solution.py:331
  39.7 8.1 %collective-permute-start.5 = (bf16[2,2,256,128]{3,2,1,0:T(8,128)(2,1)S(1)}, bf16[2,2,256,128]{3,2,1,0:T(8,128)(2,1)S(1)}, u32[]{:S(2)}, u32[]{:S(2)}) collective-permute-start(bf16[2,2,256,128]{3,2,1,0:T(8,128)(2,1)S(1)} %get-tuple-element.84), channel_id=1, source_target_pairs={{0,20},{4,16},{8,28},{12,24},{16,4},{20,0},{24,12},{28,8},{1,21},{... | collective-permute-start | bytes 786440 | tf_op jit(solution)/shard_map/ppermute | solution.py:387
  47.8 1.7 %update_items.13 = (f32[1024,1024]{1,0:T(8,128)S(1)}, f32[1024,1024]{1,0:T(8,128)S(1)}, f32[1024,1024]{1,0:T(8,128)S(1)}, f32[1024,128]{1,0:T(8,128)S(1)}, bf16[2,2,256,128]{3,2,1,0:T(8,128)(2,1)S(1)}) custom-call(s32[1]{0:T(128)} %bitcast.1.rank_ref, s32[8,32]{1,0:T(8,128)S(1)} %copy-done, ...), custom_call_target="tpu_custom_call", output_to_operand_aliasing={{0}: (7, {}), {1}: (8, {}), {2}: (9, {}), {3}: (10, {})} | custom-call | flops 1 | bytes 1 | tf_op jit(solution)/shard_map/update_items/pallas_call | solution.py:331
  49.5 3.0 %collective-permute-done.9.rest_0_ = bf16[2,4,256,128]{3,2,1,0:T(8,128)(2,1)S(1)} collective-permute-done((bf16[2,4,256,128]{3,2,1,0:T(8,128)(2,1)S(1)}, bf16[2,4,256,128]{3,2,1,0:T(8,128)(2,1)S(1)}, u32[]{:S(2)}, u32[]{:S(2)}) %collective-permute-start.9) | collective-permute-done | bytes 524320 | tf_op jit(solution)/shard_map/ppermute | solution.py:387
  52.5 1.3 %update_items.14 = (f32[1024,1024]{1,0:T(8,128)S(1)}, f32[1024,1024]{1,0:T(8,128)S(1)}, f32[1024,1024]{1,0:T(8,128)S(1)}, f32[1024,128]{1,0:T(8,128)S(1)}) custom-call(s32[1]{0:T(128)} %bitcast.1.rank_ref, s32[8,32]{1,0:T(8,128)S(1)} %copy-done, ...), custom_call_target="tpu_custom_call", output_to_operand_aliasing={{0}: (7, {}), {1}: (8, {}), {2}: (9, {}), {3}: (10, {})} | custom-call | flops 1 | bytes 1 | tf_op jit(solution)/shard_map/update_items/pallas_call | solution.py:331
  53.8 1.3 %update_items.15 = (f32[1024,1024]{1,0:T(8,128)S(1)}, f32[1024,1024]{1,0:T(8,128)S(1)}, f32[1024,1024]{1,0:T(8,128)S(1)}, f32[1024,128]{1,0:T(8,128)S(1)}) custom-call(s32[1]{0:T(128)} %bitcast.1.rank_ref, s32[8,32]{1,0:T(8,128)S(1)} %copy-done, ...), custom_call_target="tpu_custom_call", output_to_operand_aliasing={{0}: (7, {}), {1}: (8, {}), {2}: (9, {}), {3}: (10, {})} | custom-call | flops 1 | bytes 1 | tf_op jit(solution)/shard_map/update_items/pallas_call | solution.py:331
  55.1 3.0 %collective-permute-done.7.rest_0_ = bf16[2,2,256,128]{3,2,1,0:T(8,128)(2,1)S(1)} collective-permute-done((bf16[2,2,256,128]{3,2,1,0:T(8,128)(2,1)S(1)}, bf16[2,2,256,128]{3,2,1,0:T(8,128)(2,1)S(1)}, u32[]{:S(2)}, u32[]{:S(2)}) %collective-permute-start.7) | collective-permute-done | bytes 262176 | tf_op jit(solution)/shard_map/ppermute | solution.py:387
  58.1 1.1 %update_items.16 = (f32[1024,1024]{1,0:T(8,128)S(1)}, f32[1024,1024]{1,0:T(8,128)S(1)}, f32[1024,1024]{1,0:T(8,128)S(1)}, f32[1024,128]{1,0:T(8,128)S(1)}) custom-call(s32[1]{0:T(128)} %bitcast.1.rank_ref, s32[8,32]{1,0:T(8,128)S(1)} %copy-done, ...), custom_call_target="tpu_custom_call", output_to_operand_aliasing={{0}: (7, {}), {1}: (8, {}), {2}: (9, {}), {3}: (10, {})} | custom-call | flops 1 | bytes 1 | tf_op jit(solution)/shard_map/update_items/pallas_call | solution.py:331
  59.2 2.7 %collective-permute-done.6.rest_0_ = bf16[2,2,256,128]{3,2,1,0:T(8,128)(2,1)S(1)} collective-permute-done((bf16[2,2,256,128]{3,2,1,0:T(8,128)(2,1)S(1)}, bf16[2,2,256,128]{3,2,1,0:T(8,128)(2,1)S(1)}, u32[]{:S(2)}, u32[]{:S(2)}) %collective-permute-start.6) | collective-permute-done | bytes 262176 | tf_op jit(solution)/shard_map/ppermute | solution.py:387
  61.9 1.1 %update_items.17 = (f32[1024,1024]{1,0:T(8,128)S(1)}, f32[1024,1024]{1,0:T(8,128)S(1)}, f32[1024,1024]{1,0:T(8,128)S(1)}, f32[1024,128]{1,0:T(8,128)S(1)}) custom-call(s32[1]{0:T(128)} %bitcast.1.rank_ref, s32[8,32]{1,0:T(8,128)S(1)} %copy-done, ...), custom_call_target="tpu_custom_call", output_to_operand_aliasing={{0}: (7, {}), {1}: (8, {}), {2}: (9, {}), {3}: (10, {})} | custom-call | flops 1 | bytes 1 | tf_op jit(solution)/shard_map/update_items/pallas_call | solution.py:331
  63.1 0.6 collective-permute-done.5.rest_0_
  63.7 1.1 %update_items.18 = (f32[1024,1024]{1,0:T(8,128)S(1)}, f32[1024,1024]{1,0:T(8,128)S(1)}, f32[1024,1024]{1,0:T(8,128)S(1)}, f32[1024,128]{1,0:T(8,128)S(1)}) custom-call(s32[1]{0:T(128)} %bitcast.1.rank_ref, s32[8,32]{1,0:T(8,128)S(1)} %copy-done, ...), custom_call_target="tpu_custom_call", output_to_operand_aliasing={{0}: (7, {}), {1}: (8, {}), {2}: (9, {}), {3}: (10, {})} | custom-call | flops 1 | bytes 1 | tf_op jit(solution)/shard_map/update_items/pallas_call | solution.py:331
  64.8 1.4 %update_items.19 = (f32[1024,1024]{1,0:T(8,128)S(1)}, f32[1024,1024]{1,0:T(8,128)S(1)}, f32[1024,1024]{1,0:T(8,128)S(1)}, f32[1024,128]{1,0:T(8,128)S(1)}, f32[1,1024]{1,0:T(1,128)S(1)}) custom-call(s32[1]{0:T(128)} %bitcast.1.rank_ref, s32[8,32]{1,0:T(8,128)S(1)} %copy-done, ...), custom_call_target="tpu_custom_call", output_to_operand_aliasing={{0}: (7, {}), {1}: (8, {}), {2}: (9, {}), {3}: (10, {})} | custom-call | flops 1 | bytes 1 | tf_op jit(solution)/shard_map/update_items/pallas_call | solution.py:331
  66.3 2.6 %collective-permute-start.12 = (f32[1,1024]{1,0:T(1,128)S(1)}, f32[1,1024]{1,0:T(1,128)S(1)}, u32[]{:S(2)}, u32[]{:S(2)}) collective-permute-start(f32[1,1024]{1,0:T(1,128)S(1)} %get-tuple-element.113.rest_0_), channel_id=1, source_target_pairs={{0,2},{1,3},{2,0},{3,1},{4,6},{5,7},{6,4},{7,5},{8,10},{9,11},{10,... | collective-permute-start | bytes 12296 | tf_op jit(solution)/shard_map/ppermute | solution.py:409
  68.9 1.3 %collective-permute-start.11 = (f32[1,1024]{1,0:T(1,128)S(1)}, f32[1,1024]{1,0:T(1,128)S(1)}, u32[]{:S(2)}, u32[]{:S(2)}) collective-permute-start(f32[1,1024]{1,0:T(1,128)S(1)} %get-tuple-element.113.rest_0_), channel_id=1, source_target_pairs={{0,3},{1,2},{2,1},{3,0},{4,7},{5,6},{6,5},{7,4},{8,11},{9,10},{10,... | collective-permute-start | bytes 12296 | tf_op jit(solution)/shard_map/ppermute | solution.py:409
  70.3 0.2 collective-permute-start.10
  70.5 0.3 collective-permute-done.12.rest_3_
  70.8 3.5 %collective-permute-done.11.rest_2_ = f32[1,1024]{1,0:T(1,128)S(1)} collective-permute-done((f32[1,1024]{1,0:T(1,128)S(1)}, f32[1,1024]{1,0:T(1,128)S(1)}, u32[]{:S(2)}, u32[]{:S(2)}) %collective-permute-start.11) | collective-permute-done | bytes 4128 | tf_op jit(solution)/shard_map/ppermute | solution.py:409
  74.3 1.7 %scale_rows.1 = bf16[1024,1024]{1,0:T(8,128)(2,1)} custom-call(f32[1,1024]{1,0:T(1,128)S(1)} %bitcast.2, f32[1,1024]{1,0:T(1,128)S(1)} %get-tuple-element.113.rest_0_, f32[1,1024]{1,0:T(1,128)S(1)} %collective-permute-done.10.rest_1_, f32[1,1024]{1,0:T(1,128)S(1)} %collective-permute-done.11.rest_2_, f32[1,1024]{1,0:T(1,128)S(1)} %collective-permute-done.12.rest_3_, ...), custom_call_target="tpu_custom_call" | custom-call | tf_op jit(solution)/shard_map/scale_rows/pallas_call | solution.py:364
  (12 shorter events, 0.0 us)
Async XLA Ops:
  0.0 12.9 %copy-start = (s32[8,32]{1,0:T(8,128)S(1)}, s32[8,32]{1,0:T(8,128)}, u32[]{:S(2)}) copy-start(s32[8,32]{1,0:T(8,128)} %perm.21) | copy-start | bytes 3076
  1.2 22.5 %collective-permute-start.3 = (bf16[2,256,1024]{2,1,0:T(8,128)(2,1)S(1)}, bf16[2,256,1024]{2,1,0:T(8,128)(2,1)S(1)}, u32[]{:S(2)}, u32[]{:S(2)}) collective-permute-start(bf16[2,256,1024]{2,1,0:T(8,128)(2,1)S(1)} %last_blocks.1), channel_id=1, source_target_pairs={{0,4},{4,8},{8,12},{12,16},{16,20},{20,24},{24,28},{1,5},{5,9},{9,... | collective-permute-start | bytes 3145736 | tf_op jit(solution)/shard_map/previous/ppermute | solution.py:394
  6.4 21.4 %collective-permute-start.2 = (bf16[2,4,256,128]{3,2,1,0:T(8,128)(2,1)S(1)}, bf16[2,4,256,128]{3,2,1,0:T(8,128)(2,1)S(1)}, u32[]{:S(2)}, u32[]{:S(2)}) collective-permute-start(bf16[2,4,256,128]{3,2,1,0:T(8,128)(2,1)S(1)} %get-tuple-element.66), channel_id=1, source_target_pairs={{0,4},{4,0},{8,12},{12,8},{16,20},{20,16},{24,28},{28,24},{1,5},{5... | collective-permute-start | bytes 1572872 | tf_op jit(solution)/shard_map/ppermute | solution.py:387
  9.0 21.0 %collective-permute-start.1 = (bf16[2,4,256,128]{3,2,1,0:T(8,128)(2,1)S(1)}, bf16[2,4,256,128]{3,2,1,0:T(8,128)(2,1)S(1)}, u32[]{:S(2)}, u32[]{:S(2)}) collective-permute-start(bf16[2,4,256,128]{3,2,1,0:T(8,128)(2,1)S(1)} %get-tuple-element.65), channel_id=1, source_target_pairs={{0,24},{4,28},{8,16},{12,20},{16,8},{20,12},{24,0},{28,4},{1,25},{... | collective-permute-start | bytes 1572872 | tf_op jit(solution)/shard_map/ppermute | solution.py:387
  10.0 29.7 %collective-permute-start = (bf16[2,4,256,128]{3,2,1,0:T(8,128)(2,1)S(1)}, bf16[2,4,256,128]{3,2,1,0:T(8,128)(2,1)S(1)}, u32[]{:S(2)}, u32[]{:S(2)}) collective-permute-start(bf16[2,4,256,128]{3,2,1,0:T(8,128)(2,1)S(1)} %get-tuple-element.64), channel_id=1, source_target_pairs={{0,28},{4,24},{8,20},{12,16},{16,12},{20,8},{24,4},{28,0},{1,29},{... | collective-permute-start | bytes 1572872 | tf_op jit(solution)/shard_map/ppermute | solution.py:387
  11.4 41.1 %collective-permute-start.9 = (bf16[2,4,256,128]{3,2,1,0:T(8,128)(2,1)S(1)}, bf16[2,4,256,128]{3,2,1,0:T(8,128)(2,1)S(1)}, u32[]{:S(2)}, u32[]{:S(2)}) collective-permute-start(bf16[2,4,256,128]{3,2,1,0:T(8,128)(2,1)S(1)} %get-tuple-element.88), channel_id=1, source_target_pairs={{0,16},{4,20},{8,24},{12,28},{16,0},{20,4},{24,8},{28,12},{1,17},{... | collective-permute-start | bytes 1572872 | tf_op jit(solution)/shard_map/ppermute | solution.py:387
  23.7 30.1 %collective-permute-start.8 = (bf16[2,4,256,128]{3,2,1,0:T(8,128)(2,1)S(1)}, bf16[2,4,256,128]{3,2,1,0:T(8,128)(2,1)S(1)}, u32[]{:S(2)}, u32[]{:S(2)}) collective-permute-start(bf16[2,4,256,128]{3,2,1,0:T(8,128)(2,1)S(1)} %get-tuple-element.87), channel_id=1, source_target_pairs={{0,8},{4,12},{8,0},{12,4},{16,24},{20,28},{24,16},{28,20},{1,9},{5... | collective-permute-start | bytes 1572872 | tf_op jit(solution)/shard_map/ppermute | solution.py:387
  27.9 30.2 %collective-permute-start.7 = (bf16[2,2,256,128]{3,2,1,0:T(8,128)(2,1)S(1)}, bf16[2,2,256,128]{3,2,1,0:T(8,128)(2,1)S(1)}, u32[]{:S(2)}, u32[]{:S(2)}) collective-permute-start(bf16[2,2,256,128]{3,2,1,0:T(8,128)(2,1)S(1)} %get-tuple-element.86), channel_id=1, source_target_pairs={{0,20},{4,16},{8,28},{12,24},{16,4},{20,0},{24,12},{28,8},{1,21},{... | collective-permute-start | bytes 786440 | tf_op jit(solution)/shard_map/ppermute | solution.py:387
  30.0 31.9 %collective-permute-start.6 = (bf16[2,2,256,128]{3,2,1,0:T(8,128)(2,1)S(1)}, bf16[2,2,256,128]{3,2,1,0:T(8,128)(2,1)S(1)}, u32[]{:S(2)}, u32[]{:S(2)}) collective-permute-start(bf16[2,2,256,128]{3,2,1,0:T(8,128)(2,1)S(1)} %get-tuple-element.85), channel_id=1, source_target_pairs={{0,12},{4,8},{8,4},{12,0},{16,28},{20,24},{24,20},{28,16},{1,13},{... | collective-permute-start | bytes 786440 | tf_op jit(solution)/shard_map/ppermute | solution.py:387
  39.7 24.0 %collective-permute-start.5 = (bf16[2,2,256,128]{3,2,1,0:T(8,128)(2,1)S(1)}, bf16[2,2,256,128]{3,2,1,0:T(8,128)(2,1)S(1)}, u32[]{:S(2)}, u32[]{:S(2)}) collective-permute-start(bf16[2,2,256,128]{3,2,1,0:T(8,128)(2,1)S(1)} %get-tuple-element.84), channel_id=1, source_target_pairs={{0,20},{4,16},{8,28},{12,24},{16,4},{20,0},{24,12},{28,8},{1,21},{... | collective-permute-start | bytes 786440 | tf_op jit(solution)/shard_map/ppermute | solution.py:387
  52.5 12.3 %collective-permute-start.4 = (bf16[2,2,256,128]{3,2,1,0:T(8,128)(2,1)S(1)}, bf16[2,2,256,128]{3,2,1,0:T(8,128)(2,1)S(1)}, u32[]{:S(2)}, u32[]{:S(2)}) collective-permute-start(bf16[2,2,256,128]{3,2,1,0:T(8,128)(2,1)S(1)} %get-tuple-element.83), channel_id=1, source_target_pairs={{0,12},{4,8},{8,4},{12,0},{16,28},{20,24},{24,20},{28,16},{1,13},{... | collective-permute-start | bytes 786440 | tf_op jit(solution)/shard_map/ppermute | solution.py:387
  64.8 9.5 %copy-start.1 = (f32[1024]{0:T(1024)S(1)}, f32[1024]{0:T(1024)}, u32[]{:S(2)}) copy-start(f32[1024]{0:T(1024)} %param.9) | copy-start | bytes 12292
  66.3 4.6 %collective-permute-start.12 = (f32[1,1024]{1,0:T(1,128)S(1)}, f32[1,1024]{1,0:T(1,128)S(1)}, u32[]{:S(2)}, u32[]{:S(2)}) collective-permute-start(f32[1,1024]{1,0:T(1,128)S(1)} %get-tuple-element.113.rest_0_), channel_id=1, source_target_pairs={{0,2},{1,3},{2,0},{3,1},{4,6},{5,7},{6,4},{7,5},{8,10},{9,11},{10,... | collective-permute-start | bytes 12296 | tf_op jit(solution)/shard_map/ppermute | solution.py:409
  68.9 5.4 %collective-permute-start.11 = (f32[1,1024]{1,0:T(1,128)S(1)}, f32[1,1024]{1,0:T(1,128)S(1)}, u32[]{:S(2)}, u32[]{:S(2)}) collective-permute-start(f32[1,1024]{1,0:T(1,128)S(1)} %get-tuple-element.113.rest_0_), channel_id=1, source_target_pairs={{0,3},{1,2},{2,1},{3,0},{4,7},{5,6},{6,5},{7,4},{8,11},{9,10},{10,... | collective-permute-start | bytes 12296 | tf_op jit(solution)/shard_map/ppermute | solution.py:409
  70.3 4.1 %collective-permute-start.10 = (f32[1,1024]{1,0:T(1,128)S(1)}, f32[1,1024]{1,0:T(1,128)S(1)}, u32[]{:S(2)}, u32[]{:S(2)}) collective-permute-start(f32[1,1024]{1,0:T(1,128)S(1)} %get-tuple-element.113.rest_0_), channel_id=1, source_target_pairs={{0,1},{1,0},{2,3},{3,2},{4,5},{5,4},{6,7},{7,6},{8,9},{9,8},{10,11... | collective-permute-start | bytes 12296 | tf_op jit(solution)/shard_map/ppermute | solution.py:409
